TPU v7x, 128 devices: a whole 4x4x4 slice. The times are simulated.
128 devices in a mesh: drift: 16 (over z, y), cross: 8 (over x, core).
Axes of the slice: x: 4, y: 4, z: 4, core: 2. Of those that a mesh axis runs over, the one named last changes fastest.
Arguments:
- fluid_field: float32 [3, 32, 16, 1024], P(None, 'drift', 'cross'), may hold values from -6 to 6
- coords: float32 [3, 16, 8, 2048], P(None, 'drift', 'cross'), may hold values from -1 to 1
- velocity: float32 [3, 16, 8, 2048], P(None, 'drift', 'cross'), may hold values from -4 to 4
- drag_factor: float32 [16, 8, 2048], P('drift', 'cross'), may hold values from 0.05 to 0.5
- host_ids: int32 [16, 8, 2048], P('drift', 'cross'), may hold values from 0 to 7, as said below
- migrants: int32 [16, 8, 4, 512], P('drift', 'cross'), may hold values from -1 to 2047, as said below
Outputs:
- fluid_next: float32 [3, 32, 16, 1024], P(None, 'drift', 'cross')
- velocity_next: float32 [3, 16, 8, 2048], P(None, 'drift', 'cross')
Inputs may be any that keep to these rules, and one draw needn't show every extreme that they name: `host_ids`: for a particle in list d of migrants the host element lies on the layer of the neighbour tile next to the particle's own tile: x = 1 for d = 0, x = 0 for d = 1, y = 1 for d = 2, y = 0 for d = 3. `migrants`: entry [tile, d] lists in ascending order the particles of that tile hosted by neighbour d (0: one lower along drift, 1: one higher along drift, 2: one lower across, 3: one higher across), then -1 padding. A particle stands in at most one list. Every tile has one full list of 512.
All inputs are finite; a program needn't handle non-finite values.
Results may differ from a plain program's by a relative error of at most 0.0003.
Values sent between devices are 32-bit elements; how exact they have to be, the bound alone decides.
No kernel may reach another device: no remote copies, remote signals or barrier semaphores. Data moves between devices by JAX's collectives and lax.ppermute only.
A program may use at most 64 MiB of HBM per device.

v0:
```python
import math

import jax
import jax.numpy as jnp
import numpy as np
from jax import lax
from jax.sharding import PartitionSpec as P

mass_ratio = 4.0
diffusion_rate = 0.002
penalty_rate = 0.05


def extended(cells, sides, width):
    for axis, dim in sides:
        count = lax.axis_size(axis)
        head = lax.slice_in_dim(cells, 0, width, axis=dim)
        tail = lax.slice_in_dim(cells, cells.shape[dim] - width, cells.shape[dim], axis=dim)
        cells = jnp.concatenate(
            [
                lax.ppermute(tail, axis, [(i, (i + 1) % count) for i in range(count)]),
                cells,
                lax.ppermute(head, axis, [((i + 1) % count, i) for i in range(count)]),
            ],
            axis=dim,
        )
    return cells


def shifted(block, axis, distance):
    devices = range(lax.axis_size(axis))
    route = [((i - distance) % len(devices), i) for i in devices]
    return lax.ppermute(block, axis, route)


def node_points():
    counter = jnp.arange(8, dtype=jnp.float32)
    return -jnp.cos(jnp.pi * counter / 7.0)


def lagrange_rows(points):
    nodes_all = node_points()
    rows_out = []
    for target in range(8):
        numerator = jnp.ones_like(points)
        denominator = jnp.ones((), jnp.float32)
        for partner in range(8):
            if partner != target:
                numerator = numerator * (points - nodes_all[partner])
                denominator = denominator * (nodes_all[target] - nodes_all[partner])
        rows_out.append(numerator / denominator)
    return jnp.stack(rows_out, axis=0)


def node_weights(coords):
    weight_drift = lagrange_rows(coords[0])
    weight_cross = lagrange_rows(coords[1])
    weight_depth = lagrange_rows(coords[2])
    joined = (
        weight_drift[:, None, None, :]
        * weight_cross[None, :, None, :]
        * weight_depth[None, None, :, :]
    )
    return joined.reshape(512, -1).T


def couple_rows(element_table, coords, velocity, drag_factor, host_ids):
    usable = host_ids >= 0
    safe_rows = jnp.where(usable, host_ids, 0)
    weights = node_weights(coords)
    sampled = element_table[:, safe_rows, :]
    carried = jnp.sum(sampled * weights[None], axis=2)
    slip_speed = carried - velocity
    updated = velocity + drag_factor[None] * slip_speed
    reaction = jnp.where(usable[None], -mass_ratio * drag_factor[None] * slip_speed, 0.0)
    spread = reaction[:, :, None] * weights[None]
    return (updated, spread, safe_rows)


def scan_rows(element_table, coords, velocity, drag_factor, host_ids, elements):
    row_count = host_ids.shape[0]
    block_rows = math.gcd(row_count, 1024)
    block_count = row_count // block_rows

    def visit(deposit, pieces):
        piece_coords, piece_velocity, piece_drag, piece_hosts = pieces
        updated, spread, safe_rows = couple_rows(
            element_table, piece_coords, piece_velocity, piece_drag, piece_hosts
        )
        return (deposit.at[:, safe_rows, :].add(spread), updated)

    pieces = (
        coords.reshape(3, block_count, block_rows).transpose(1, 0, 2),
        velocity.reshape(3, block_count, block_rows).transpose(1, 0, 2),
        drag_factor.reshape(block_count, block_rows),
        host_ids.reshape(block_count, block_rows),
    )
    start = jnp.zeros((3, elements, 512), jnp.float32)
    deposit, updated = lax.scan(visit, start, pieces)
    return (deposit, updated.transpose(1, 0, 2).reshape(3, row_count))


def hop_codes(migrant_rows, particle_count):
    codes_out = jnp.zeros((particle_count,), jnp.int32)
    for direction in range(4):
        entries = migrant_rows[direction]
        targets = jnp.where(entries < 0, particle_count, entries)
        codes_out = codes_out.at[targets].set(direction + 1, mode="drop")
    return codes_out


def second_derivative():
    nodes_all = node_points()
    row_index = jnp.arange(8)[:, None]
    column_index = jnp.arange(8)[None, :]
    end_scale = jnp.where((jnp.arange(8) == 0) | (jnp.arange(8) == 7), 2.0, 1.0).astype(jnp.float32)
    sign_table = jnp.where((row_index + column_index) % 2 == 0, 1.0, -1.0).astype(jnp.float32)
    node_gaps = nodes_all[:, None] - nodes_all[None, :] + jnp.eye(8, dtype=jnp.float32)
    off_diagonal = end_scale[:, None] / end_scale[None, :] * sign_table / node_gaps
    off_diagonal = jnp.where(row_index == column_index, 0.0, off_diagonal)
    derivative = off_diagonal - jnp.diag(jnp.sum(off_diagonal, axis=1))
    return jnp.dot(derivative, derivative, precision=lax.Precision.HIGHEST)


def operator_transposed():
    second = second_derivative()
    ident = jnp.eye(8, dtype=jnp.float32)
    full = (
        jnp.kron(jnp.kron(second, ident), ident)
        + jnp.kron(jnp.kron(ident, second), ident)
        + jnp.kron(jnp.kron(ident, ident), second)
    )
    return full.T


def face_tables():
    side_table = np.zeros((512, 256), np.float32)
    depth_table = np.zeros((512, 128), np.float32)
    multiple = np.zeros((512,), np.float32)
    for first in range(8):
        for second_index in range(8):
            inner = first * 8 + second_index
            side_table[0 * 64 + first * 8 + second_index, inner] = 1.0
            side_table[7 * 64 + first * 8 + second_index, 64 + inner] = 1.0
            side_table[first * 64 + 0 * 8 + second_index, 128 + inner] = 1.0
            side_table[first * 64 + 7 * 8 + second_index, 192 + inner] = 1.0
            depth_table[first * 64 + second_index * 8 + 0, inner] = 1.0
            depth_table[first * 64 + second_index * 8 + 7, 64 + inner] = 1.0
    for point in range(512):
        coords_here = (point // 64, point // 8 % 8, point % 8)
        multiple[point] = float(sum((1 for value in coords_here if value in (0, 7))))
    return (jnp.asarray(side_table), jnp.asarray(depth_table), jnp.asarray(multiple))


def per_device(fluid_field, coords, velocity, drag_factor, host_ids, migrants):
    tile_x = fluid_field.shape[1]
    tile_y = fluid_field.shape[2]
    layers = fluid_field.shape[3] // 512
    particle_count = host_ids.shape[-1]
    own_coords = coords.reshape(3, particle_count)
    own_velocity = velocity.reshape(3, particle_count)
    own_drag = drag_factor.reshape(particle_count)
    own_hosts = host_ids.reshape(particle_count)
    migrant_rows = migrants.reshape(4, -1)
    hop = hop_codes(migrant_rows, particle_count)
    highest = lax.Precision.HIGHEST
    padded_field = extended(fluid_field, (("drift", 1), ("cross", 2)), 1)
    along_drift = own_hosts // (tile_y * layers) + 1
    along_cross = own_hosts // layers % tile_y + 1
    along_depth = own_hosts % layers
    along_drift = along_drift + jnp.where(hop == 1, -tile_x, jnp.where(hop == 2, tile_x, 0))
    along_cross = along_cross + jnp.where(hop == 3, -tile_y, jnp.where(hop == 4, tile_y, 0))
    extended_ids = (along_drift * (tile_y + 2) + along_cross) * layers + along_depth
    ghost_table = padded_field.reshape(3, -1, 512)
    extended_count = (tile_x + 2) * (tile_y + 2) * layers
    deposit, velocity_rows = scan_rows(
        ghost_table, own_coords, own_velocity, own_drag, extended_ids, extended_count
    )
    deposit = deposit.reshape(3, tile_x + 2, tile_y + 2, layers * 512)
    inner = deposit[:, 1:-1, 1:-1]
    for rim_index, shift_by, layer_index in ((0, -1, tile_x - 1), (tile_x + 1, 1, 0)):
        received = shifted(deposit[:, rim_index, 1:-1], "drift", shift_by)
        inner = inner.at[:, layer_index].add(received)
    for rim_index, shift_by, layer_index in ((0, -1, tile_y - 1), (tile_y + 1, 1, 0)):
        received = shifted(deposit[:, 1:-1, rim_index], "cross", shift_by)
        inner = inner.at[:, :, layer_index].add(received)
    side_table, depth_table, multiple = face_tables()
    operator_t = operator_transposed()
    deposit_grid = inner.reshape(3, tile_x, tile_y, layers, 512)
    field_state = fluid_field.reshape(3, tile_x, tile_y, layers, 512)
    for substep in range(2):
        side_faces = jnp.dot(field_state, side_table, precision=highest)
        face_stack = side_faces.reshape(3, tile_x, tile_y, layers * 256)
        padded = extended(face_stack, (("drift", 1), ("cross", 2)), 1)
        padded = padded.reshape(3, tile_x + 2, tile_y + 2, layers, 256)
        below_x = padded[:, :-2, 1:-1, :, 64:128]
        above_x = padded[:, 2:, 1:-1, :, 0:64]
        below_y = padded[:, 1:-1, :-2, :, 192:256]
        above_y = padded[:, 1:-1, 2:, :, 128:192]
        incoming = jnp.concatenate([below_x, above_x, below_y, above_y], axis=4)
        depth_faces = jnp.dot(field_state, depth_table, precision=highest)
        wall_zeros = jnp.zeros((3, tile_x, tile_y, 1, 64), jnp.float32)
        below_z = jnp.concatenate([wall_zeros, depth_faces[:, :, :, :-1, 64:128]], axis=3)
        above_z = jnp.concatenate([depth_faces[:, :, :, 1:, 0:64], wall_zeros], axis=3)
        incoming_depth = jnp.concatenate([below_z, above_z], axis=4)
        face_sum = (
            jnp.dot(incoming, side_table.T, precision=highest)
            + jnp.dot(incoming_depth, depth_table.T, precision=highest)
            - field_state * multiple
        )
        rate_now = (
            diffusion_rate * jnp.dot(field_state, operator_t, precision=highest)
            + penalty_rate * face_sum
        )
        field_state = field_state + rate_now + 0.5 * deposit_grid
    fluid_next = field_state.reshape(3, tile_x, tile_y, layers * 512)
    velocity_next = velocity_rows.reshape(3, 1, 1, particle_count)
    return (fluid_next, velocity_next)


def solution(mesh):
    placed = (
        P(None, "drift", "cross", None),
        P(None, "drift", "cross", None),
        P(None, "drift", "cross", None),
        P("drift", "cross", None),
        P("drift", "cross", None),
        P("drift", "cross", None, None),
    )
    return jax.shard_map(
        per_device,
        mesh=mesh,
        in_specs=placed,
        out_specs=(P(None, "drift", "cross", None), P(None, "drift", "cross", None)),
        check_vma=False,
    )
```

profile of v0, /device:TPU:1, one launch (start us, length us, event | category | flops | bytes accessed | tf_op | source)
XLA Modules:
  0.0 487.7 jit_solution(10725319213682770654)
XLA Ops:
  1.5 1.5 convolution_bitcast_fusion
  3.0 2.2 collective-permute-start
  5.2 5.0 %collective-permute-start.1 = (f32[3,1,2,512]{3,2,1,0:T(2,128)S(1)}, f32[3,1,2,512]{3,2,1,0:T(2,128)S(1)}, u32[]{:S(2)}, u32[]{:S(2)}) collective-permute-start(f32[3,1,2,512]{3,2,1,0:T(2,128)S(1)} %get-tuple-element.255), channel_id=1, source_target_pairs={{8,0},{16,8},{24,16},{32,24},{40,32},{48,40},{56,48},{64,56},{72,6... | collective-permute-start | bytes 36872 | tf_op jit(solution)/shard_map/ppermute | solution.py:23
  11.0 4.8 collective-permute-start.5
  15.8 1.3 convolution_bitcast_fusion.1
  18.8 6.6 %multiply_add_fusion = f32[64,8,64,8]{3,2,1,0:T(8,128)} fusion(f32[64,64]{1,0:T(8,128)S(1)} %reshape.2017, f32[8,8]{1,0:T(8,128)S(1)} %fusion.86, f32[64,64]{1,0:T(8,128)S(1)} %mul.2350, f32[8,8]{1,0:T(8,128)S(1)} %fusion.82), kind=kLoop, calls=%fused_computation.168 | loop fusion | flops 786432 | bytes 1081856 | tf_op jit(solution)/shard_map/add | solution.py:129
  25.4 2.4 scatter_custom_fusion.1
  27.9 2.5 scatter_fusion.1
  30.4 2.5 scatter_fusion.2
  32.9 2.6 scatter_fusion.3
  35.7 13.5 %reshape.2066 = f32[512,512,1,1,1]{1,0,2,3,4:T(8,128)} reshape(f32[64,8,64,8]{3,2,1,0:T(8,128)} %multiply_add_fusion) | data formatting | bytes 2097152 | tf_op jit(solution)/shard_map/add | solution.py:129
  50.5 1.3 copy.60
  51.9 1.5 collective-permute-start.3
  53.5 1.1 collective-permute-start.2
  55.0 1.5 collective-permute-start.6
  57.4 1.0 fusion.46
  59.1 398.6 %while.18 = (s32[]{:T(128)}, f32[3,32,512]{2,0,1:T(4,128)S(1)}, f32[2,3,1024]{1,2,0:T(8,128)}, s32[2,1024]{1,0:T(2,128)S(1)}, f32[2,1024]{1,0:T(2,128)S(1)}, /*i...) while((s32[]{:T(128)}, f32[3,32,512]{2,0,1:T(4,128)S(1)}, ...), condition=%wide.region_8.9_spmd, body=%wide.region_5.8_spmd.sunk | while | flops 7096444 | bytes 57482972 | solution.py:99
  59.1 13.2 %gather_fusion = f32[1024,3,512]{2,1,0:T(4,128)} fusion(f32[3,32,512]{2,0,1:T(4,128)S(1)} %get-tuple-element.421, s32[1024]{0:T(1024)S(1)} %broadcast_clamp_fusion.2), kind=kCustom, calls=%fused_computation.clone.1 | custom fusion | bytes 12587008 | tf_op jit(solution)/shard_map/while/body/eval_jaxpr/gather | solution.py:71
  99.9 5.1 %fusion.142 = (f32[1,1024]{1,0:T(1,128)S(1)}, f32[1,1024]{1,0:T(1,128)S(1)}, f32[1,1024]{1,0:T(1,128)S(1)}, f32[1,1024]{1,0:T(1,128)S(1)}, f32[1,1024]{1,0:T(1,1...) fusion(f32[]{:T(128)S(6)} %mul.2929, f32[]{:T(128)} %bitcast.642, ...), kind=kLoop, calls=%fused_computation.131.clone.1 | loop fusion | flops 74752 | bytes 45112 | tf_op jit(solution)/shard_map/while/body/eval_jaxpr/div | solution.py:51
  148.5 5.1 %fusion.143 = (f32[1,1024]{1,0:T(1,128)S(1)}, f32[1,1024]{1,0:T(1,128)S(1)}, f32[1,1024]{1,0:T(1,128)S(1)}, f32[1,1024]{1,0:T(1,128)S(1)}, f32[1,1024]{1,0:T(1,1...) fusion(f32[]{:T(128)S(6)} %mul.2947, ...), kind=kLoop, calls=%fused_computation.123.clone.1 | loop fusion | flops 86016 | bytes 69700 | tf_op jit(solution)/shard_map/while/body/eval_jaxpr/div | solution.py:51
  153.6 2.4 fusion.144
  156.3 1.7 broadcast_multiply_fusion.8
  157.9 1.9 copy.121
  159.9 5.7 %multiply_reduce_fusion.2 = f32[1024,3]{1,0:T(8,128)S(1)} fusion(f32[1024,3,512]{2,1,0:T(4,128)} %gather_fusion, f32[1024,512]{1,0:T(8,128)S(1)} %copy.121), kind=kLoop, calls=%fused_computation.6.clone.1 | loop fusion | flops 3142656 | bytes 8400896 | tf_op jit(solution)/shard_map/while/body/eval_jaxpr/reduce_sum | solution.py:72
  165.6 1.4 fusion.145
  167.0 4.3 multiply_bitcast_fusion.2
  171.3 85.9 %scatter_fusion = f32[3,32,512]{2,0,1:T(4,128)S(1)} fusion(f32[3,32,512]{2,0,1:T(4,128)S(1)} %get-tuple-element.405, s32[1024]{0:T(1024)S(1)} %bitcast.651, f32[1024,3,512]{2,1,0:T(4,128)} %multiply_bitcast_fusion.2), kind=kCustom, calls=%fused_computation.1.clone.1 | custom fusion | flops 1572864 | bytes 18878464 | tf_op jit(solution)/shard_map/while/body/eval_jaxpr/scatter-add | solution.py:90
  257.5 1.0 copy-done.4
  258.4 13.2 %gather_fusion = f32[1024,3,512]{2,1,0:T(4,128)} fusion(f32[3,32,512]{2,0,1:T(4,128)S(1)} %get-tuple-element.421, s32[1024]{0:T(1024)S(1)} %broadcast_clamp_fusion.2), kind=kCustom, calls=%fused_computation.clone.1 | custom fusion | bytes 12587008 | tf_op jit(solution)/shard_map/while/body/eval_jaxpr/gather | solution.py:71
  299.2 5.1 %fusion.142 = (f32[1,1024]{1,0:T(1,128)S(1)}, f32[1,1024]{1,0:T(1,128)S(1)}, f32[1,1024]{1,0:T(1,128)S(1)}, f32[1,1024]{1,0:T(1,128)S(1)}, f32[1,1024]{1,0:T(1,1...) fusion(f32[]{:T(128)S(6)} %mul.2929, f32[]{:T(128)} %bitcast.642, ...), kind=kLoop, calls=%fused_computation.131.clone.1 | loop fusion | flops 74752 | bytes 45112 | tf_op jit(solution)/shard_map/while/body/eval_jaxpr/div | solution.py:51
  347.8 5.1 %fusion.143 = (f32[1,1024]{1,0:T(1,128)S(1)}, f32[1,1024]{1,0:T(1,128)S(1)}, f32[1,1024]{1,0:T(1,128)S(1)}, f32[1,1024]{1,0:T(1,128)S(1)}, f32[1,1024]{1,0:T(1,1...) fusion(f32[]{:T(128)S(6)} %mul.2947, ...), kind=kLoop, calls=%fused_computation.123.clone.1 | loop fusion | flops 86016 | bytes 69700 | tf_op jit(solution)/shard_map/while/body/eval_jaxpr/div | solution.py:51
  352.9 2.4 fusion.144
  355.6 1.7 broadcast_multiply_fusion.8
  357.3 1.9 copy.121
  359.2 5.7 %multiply_reduce_fusion.2 = f32[1024,3]{1,0:T(8,128)S(1)} fusion(f32[1024,3,512]{2,1,0:T(4,128)} %gather_fusion, f32[1024,512]{1,0:T(8,128)S(1)} %copy.121), kind=kLoop, calls=%fused_computation.6.clone.1 | loop fusion | flops 3142656 | bytes 8400896 | tf_op jit(solution)/shard_map/while/body/eval_jaxpr/reduce_sum | solution.py:72
  364.9 1.4 fusion.145
  366.3 4.3 multiply_bitcast_fusion.2
  370.6 85.9 %scatter_fusion = f32[3,32,512]{2,0,1:T(4,128)S(1)} fusion(f32[3,32,512]{2,0,1:T(4,128)S(1)} %get-tuple-element.405, s32[1024]{0:T(1024)S(1)} %bitcast.651, f32[1024,3,512]{2,1,0:T(4,128)} %multiply_bitcast_fusion.2), kind=kCustom, calls=%fused_computation.1.clone.1 | custom fusion | flops 1572864 | bytes 18878464 | tf_op jit(solution)/shard_map/while/body/eval_jaxpr/scatter-add | solution.py:90
  456.7 1.0 copy-done.4
  458.1 1.5 collective-permute-start.9
  459.6 4.4 collective-permute-start.10
  464.1 2.2 copy.85
  467.1 2.4 fusion.44
  469.5 1.4 fusion.122
  471.4 4.8 collective-permute-start.13
  477.1 4.1 collective-permute-start.15
  482.7 1.6 fusion.54
  484.7 2.3 fusion.40
  (149 shorter events, 14.1 us)
Async XLA Ops:
  3.0 48.8 %collective-permute-start = (f32[3,1,2,512]{3,2,1,0:T(2,128)S(1)}, f32[3,1,2,512]{3,2,1,0:T(2,128)S(1)}, u32[]{:S(2)}, u32[]{:S(2)}) collective-permute-start(f32[3,1,2,512]{3,2,1,0:T(2,128)S(1)} %get-tuple-element.256), channel_id=1, source_target_pairs={{0,8},{8,16},{16,24},{24,32},{32,40},{40,48},{48,56},{56,64},{64,7... | collective-permute-start | bytes 36872 | tf_op jit(solution)/shard_map/ppermute | solution.py:21
  5.2 46.6 %collective-permute-start.1 = (f32[3,1,2,512]{3,2,1,0:T(2,128)S(1)}, f32[3,1,2,512]{3,2,1,0:T(2,128)S(1)}, u32[]{:S(2)}, u32[]{:S(2)}) collective-permute-start(f32[3,1,2,512]{3,2,1,0:T(2,128)S(1)} %get-tuple-element.255), channel_id=1, source_target_pairs={{8,0},{16,8},{24,16},{32,24},{40,32},{48,40},{56,48},{64,56},{72,6... | collective-permute-start | bytes 36872 | tf_op jit(solution)/shard_map/ppermute | solution.py:23
  11.0 43.6 %collective-permute-start.4 = (f32[3,1,2,1024]{3,2,1,0:T(2,128)S(1)}, f32[3,1,2,1024]{3,2,1,0:T(2,128)S(1)}, u32[]{:S(2)}, u32[]{:S(2)}) collective-permute-start(f32[3,1,2,1024]{3,2,1,0:T(2,128)S(1)} %get-tuple-element.250), channel_id=1, source_target_pairs={{0,8},{8,16},{16,24},{24,32},{32,40},{40,48},{48,56},{56,64},{64,7... | collective-permute-start | bytes 73736 | tf_op jit(solution)/shard_map/ppermute | solution.py:21
  11.0 43.6 %collective-permute-start.5 = (f32[3,1,2,1024]{3,2,1,0:T(2,128)S(1)}, f32[3,1,2,1024]{3,2,1,0:T(2,128)S(1)}, u32[]{:S(2)}, u32[]{:S(2)}) collective-permute-start(f32[3,1,2,1024]{3,2,1,0:T(2,128)S(1)} %get-tuple-element.249), channel_id=1, source_target_pairs={{8,0},{16,8},{24,16},{32,24},{40,32},{48,40},{56,48},{64,56},{72,6... | collective-permute-start | bytes 73736 | tf_op jit(solution)/shard_map/ppermute | solution.py:23
  25.4 10.1 %copy-start.9 = (s32[1,1,2048]{2,1,0:T(1,128)S(1)}, s32[1,1,2048]{2,1,0:T(1,128)}, u32[]{:S(2)}) copy-start(s32[1,1,2048]{2,1,0:T(1,128)} %param.23) | copy-start | bytes 24580
  35.6 14.1 %copy-start.10 = (f32[1,1,2048]{2,1,0:T(1,128)S(1)}, f32[1,1,2048]{2,1,0:T(1,128)}, u32[]{:S(2)}) copy-start(f32[1,1,2048]{2,1,0:T(1,128)} %param.22) | copy-start | bytes 24580
  35.6 14.8 %copy-start.6 = (f32[3,1,1,2048]{3,2,1,0:T(1,128)S(1)}, f32[3,1,1,2048]{3,2,1,0:T(1,128)}, u32[]{:S(2)}) copy-start(f32[3,1,1,2048]{3,2,1,0:T(1,128)} %param.20) | copy-start | bytes 73732
  35.6 14.9 %copy-start.7 = (f32[3,1,1,2048]{3,2,1,0:T(1,128)S(1)}, f32[3,1,1,2048]{3,2,1,0:T(1,128)}, u32[]{:S(2)}) copy-start(f32[3,1,1,2048]{3,2,1,0:T(1,128)} %param.21) | copy-start | bytes 73732
  35.6 19.0 %copy-start.5 = (f32[3,2,2,1024]{3,2,1,0:T(2,128)S(1)}, f32[3,2,2,1024]{3,2,1,0:T(2,128)}, u32[]{:S(2)}) copy-start(f32[3,2,2,1024]{3,2,1,0:T(2,128)} %param.19) | copy-start | bytes 147460
  35.6 21.2 %copy-start.1 = (f32[512,256,1,1,1]{1,0,4,3,2:T(8,128)S(1)}, f32[512,256,1,1,1]{1,0,4,3,2:T(8,128)}, u32[]{:S(2)}) copy-start(f32[512,256,1,1,1]{1,0,4,3,2:T(8,128)} %constant.271) | copy-start | bytes 1572868
  35.6 21.8 %copy-start.2 = (f32[512,128,1,1,1]{1,0,4,3,2:T(8,128)S(1)}, f32[512,128,1,1,1]{1,0,4,3,2:T(8,128)}, u32[]{:S(2)}) copy-start(f32[512,128,1,1,1]{1,0,4,3,2:T(8,128)} %constant.272) | copy-start | bytes 786436
  35.6 21.8 %copy-start.8 = (f32[512]{0:T(512)S(1)}, f32[512]{0:T(512)}, u32[]{:S(2)}) copy-start(f32[512]{0:T(512)} %constant.256.clone) | copy-start | bytes 6148
  51.9 4.5 collective-permute-start.3
  53.5 3.0 collective-permute-start.2
  54.7 3.8 collective-permute-start.7
  55.0 3.7 collective-permute-start.6
  171.3 86.0 %copy-start = (f32[2,3,1024]{1,2,0:T(8,128)S(1)}, f32[2,3,1024]{1,2,0:T(8,128)}, u32[]{:S(2)}) copy-start(f32[2,3,1024]{1,2,0:T(8,128)} %get-tuple-element.423) | copy-start | bytes 73732 | tf_op jit(solution)/shard_map/while
  171.3 86.0 %copy-start.3 = (f32[2,3,1024]{1,2,0:T(8,128)S(1)}, f32[2,3,1024]{1,2,0:T(8,128)}, u32[]{:S(2)}) copy-start(f32[2,3,1024]{1,2,0:T(8,128)} %get-tuple-element.406) | copy-start | bytes 73732 | tf_op jit(solution)/shard_map/while
  257.4 1.0 copy-start.4
  370.6 85.9 %copy-start = (f32[2,3,1024]{1,2,0:T(8,128)S(1)}, f32[2,3,1024]{1,2,0:T(8,128)}, u32[]{:S(2)}) copy-start(f32[2,3,1024]{1,2,0:T(8,128)} %get-tuple-element.423) | copy-start | bytes 73732 | tf_op jit(solution)/shard_map/while
  370.6 85.9 %copy-start.3 = (f32[2,3,1024]{1,2,0:T(8,128)S(1)}, f32[2,3,1024]{1,2,0:T(8,128)}, u32[]{:S(2)}) copy-start(f32[2,3,1024]{1,2,0:T(8,128)} %get-tuple-element.406) | copy-start | bytes 73732 | tf_op jit(solution)/shard_map/while
  456.7 1.0 copy-start.4
  457.9 8.4 %collective-permute-start.8 = (f32[3,2,1024]{2,1,0:T(2,128)S(1)}, f32[3,2,1024]{2,1,0:T(2,128)S(1)}, u32[]{:S(2)}, u32[]{:S(2)}) collective-permute-start(f32[3,2,1024]{2,1,0:T(2,128)S(1)} %get-tuple-element.236), channel_id=1, source_target_pairs={{8,0},{16,8},{24,16},{32,24},{40,32},{48,40},{56,48},{64,56},{72,6... | collective-permute-start | bytes 73736 | tf_op jit(solution)/shard_map/ppermute | solution.py:33
  458.1 8.4 %collective-permute-start.9 = (f32[3,2,1024]{2,1,0:T(2,128)S(1)}, f32[3,2,1024]{2,1,0:T(2,128)S(1)}, u32[]{:S(2)}, u32[]{:S(2)}) collective-permute-start(f32[3,2,1024]{2,1,0:T(2,128)S(1)} %get-tuple-element.234), channel_id=1, source_target_pairs={{120,0},{0,8},{8,16},{16,24},{24,32},{32,40},{40,48},{48,56},{56,6... | collective-permute-start | bytes 73736 | tf_op jit(solution)/shard_map/ppermute | solution.py:33
  459.6 7.3 %collective-permute-start.10 = (f32[3,2,1024]{2,1,0:T(2,128)S(1)}, f32[3,2,1024]{2,1,0:T(2,128)S(1)}, u32[]{:S(2)}, u32[]{:S(2)}) collective-permute-start(f32[3,2,1024]{2,1,0:T(2,128)S(1)} %bitcast.654), channel_id=1, source_target_pairs={{1,0},{2,1},{3,2},{4,3},{5,4},{6,5},{7,6},{0,7},{9,8},{10,9},{11,1... | collective-permute-start | bytes 73736 | tf_op jit(solution)/shard_map/ppermute | solution.py:33
  464.1 2.9 collective-permute-start.11
  471.0 5.9 %collective-permute-start.12 = (f32[3,1,2,512]{3,2,1,0:T(2,128)S(1)}, f32[3,1,2,512]{3,2,1,0:T(2,128)S(1)}, u32[]{:S(2)}, u32[]{:S(2)}) collective-permute-start(f32[3,1,2,512]{3,2,1,0:T(2,128)S(1)} %get-tuple-element.254), channel_id=1, source_target_pairs={{0,8},{8,16},{16,24},{24,32},{32,40},{40,48},{48,56},{56,64},{64,7... | collective-permute-start | bytes 36872 | tf_op jit(solution)/shard_map/ppermute | solution.py:21
  471.4 5.7 %collective-permute-start.13 = (f32[3,1,2,512]{3,2,1,0:T(2,128)S(1)}, f32[3,1,2,512]{3,2,1,0:T(2,128)S(1)}, u32[]{:S(2)}, u32[]{:S(2)}) collective-permute-start(f32[3,1,2,512]{3,2,1,0:T(2,128)S(1)} %get-tuple-element.253), channel_id=1, source_target_pairs={{8,0},{16,8},{24,16},{32,24},{40,32},{48,40},{56,48},{64,56},{72,6... | collective-permute-start | bytes 36872 | tf_op jit(solution)/shard_map/ppermute | solution.py:23
  477.1 4.9 %collective-permute-start.15 = (f32[3,4,1,512]{3,2,1,0:T(1,128)S(1)}, f32[3,4,1,512]{3,2,1,0:T(1,128)S(1)}, u32[]{:S(2)}, u32[]{:S(2)}) collective-permute-start(f32[3,4,1,512]{3,2,1,0:T(1,128)S(1)} %get-tuple-element.248), channel_id=1, source_target_pairs={{1,0},{2,1},{3,2},{4,3},{5,4},{6,5},{7,6},{0,7},{9,8},{10,9},{11,1... | collective-permute-start | bytes 73736 | tf_op jit(solution)/shard_map/ppermute | solution.py:23
  481.2 1.2 collective-permute-start.14
where the time goes:
time: 495 us; the launch traced here: 488 us
  other arithmetic  233 us (47%)
  loops' own time  141 us (28%)
  local copies, waits for them, and re-layouts  66.3 us (13%)
  starting transfers between devices  31.4 us (6%)
  matrix products  12.9 us (3%)
    scatter-add x2, other arithmetic, visit(): return (deposit.at[:, safe_rows, :].add(spread), updated)  172 us
    another operation x1, loops' own time, scan_rows(): deposit, updated = lax.scan(visit, start, pieces)  141 us
    gather x2, local copies, waits for them, and re-layouts, couple_rows(): sampled = element_table[:, safe_rows, :]  26.5 us
    div x6, other arithmetic, lagrange_rows(): rows_out.append(numerator / denominator)  25.3 us
    ppermute x6, starting transfers between devices, extended(): lax.ppermute(head, axis, [((i + 1) % count, i) for i in range(count)])  20.5 us
    add x1, local copies, waits for them, and re-layouts, operator_transposed(): jnp.kron(jnp.kron(second, ident), ident)  13.5 us
    reduce_sum x2, other arithmetic, couple_rows(): carried = jnp.sum(sampled * weights[None], axis=2)  11.3 us
    scatter x4, local copies, waits for them, and re-layouts, hop_codes(): codes_out = codes_out.at[targets].set(direction + 1, mode='drop')  10 us
  transfers between devices with their start and end apart: 16, of which 6 were waited for; matrix products, arithmetic and copies ran while one was open for 9% of the time, Pallas kernels for 0%

commit v1 on v0

v1 whole, which is shorter than its diff:
```python
import functools

import jax
import jax.numpy as jnp
import numpy as np
from jax import lax
from jax.experimental import pallas as pl
from jax.experimental.pallas import tpu as pltpu
from jax.sharding import PartitionSpec as P


F32 = jnp.float32
BF16 = jnp.bfloat16
MASS = 4.0
DIFF = 0.002
PEN = 0.05
VMEM = 24 << 20

NODES = -np.cos(np.pi * np.arange(8) / 7.0)
DENOM = np.array([np.prod([NODES[t] - NODES[m] for m in range(8) if m != t]) for t in range(8)])


def second_np():
    end = np.where((np.arange(8) == 0) | (np.arange(8) == 7), 2.0, 1.0)
    d = np.zeros((8, 8))
    for i in range(8):
        for m in range(8):
            if i != m:
                d[i, m] = end[i] / end[m] * (-1.0) ** (i + m) / (NODES[i] - NODES[m])
    d -= np.diag(d.sum(axis=1))
    return d @ d


def operator_tables():
    s = second_np()
    tab = np.zeros((2, 4, 8, 128))
    a1 = np.arange(128) // 64
    b = np.arange(128) // 8 % 8
    k = np.arange(128) % 8
    for sub in range(8):
        a2 = sub // 2
        a = 2 * a2 + a1
        for step in range(4):
            other = (a2 - step) % 4
            tab[0, step, sub] = DIFF * s[a, 2 * other + a1]
            tab[1, step, sub] = DIFF * s[a, 2 * other + 1 - a1]
        mult = ((a == 0) | (a == 7)) * 1.0 + ((b == 0) | (b == 7)) + ((k == 0) | (k == 7))
        tab[0, 0, sub] += 1.0 - PEN * mult
    eye = np.eye(8)
    side = DIFF * (np.kron(s, eye) + np.kron(eye, s))
    lane = np.kron(np.eye(2), side).T.astype(np.float32)
    hi = lane.astype(jnp.bfloat16)
    lo = (lane - hi.astype(np.float32)).astype(jnp.bfloat16)
    half = np.concatenate([hi, lo], axis=1)
    return tab.reshape(64, 128).astype(np.float32), np.concatenate([half, half], axis=0)


def iota(shape, dim):
    return lax.broadcasted_iota(jnp.int32, shape, dim)


def split(x):
    hi = x.astype(BF16)
    lo = (x - hi.astype(F32)).astype(BF16)
    return hi, lo


def row_of(ref, r):
    return jnp.broadcast_to(ref[r : r + 1, :], (8, 128))


def sublane_table(values):
    sub = iota((8, 128), 0)
    out = jnp.full((8, 128), float(values[0]), F32)
    for i in range(1, 8):
        out = jnp.where(sub == i, float(values[i]), out)
    return out


def node_tables(order):
    partners = [[m for m in range(8) if m != t] for t in order]
    tables = [sublane_table([NODES[p[j]] for p in partners]) for j in range(7)]
    return tables, sublane_table([1.0 / DENOM[t] for t in order])


def lagrange(s, tables):
    nodes, scale = tables
    out = (s - nodes[0]) * scale
    for t in nodes[1:]:
        out = out * (s - t)
    return out


def tile_of(ref, c, x, z):
    r = ((c * 2 + x) * 2 + z) * 8
    return ref[r : r + 8, :]


CXZ = [(c, x, z) for c in range(3) for x in range(2) for z in range(2)]


def parity(axis):
    return lax.rem(lax.axis_index(axis), 2) == 1


def face_masks():
    sub, lane = iota((8, 128), 0), iota((8, 128), 1)
    a2, y, a1, b, k = sub // 2, sub % 2, lane // 64, lane // 8 % 8, lane % 8
    pick = lambda cond: jnp.where(cond, PEN, 0.0).astype(F32)
    return dict(
        x_lo=pick((a2 == 0) & (a1 == 0)),
        x_hi=pick((a2 == 3) & (a1 == 1)),
        y_lo=pick((y == 0) & (b == 0)),
        y_hi=pick((y == 1) & (b == 7)),
        y_in_hi=pick((y == 0) & (b == 7)),
        y_in_lo=pick((y == 1) & (b == 0)),
        z_lo=pick(k == 0),
        z_hi=pick(k == 7),
    )


def pack_faces(get):
    lane = iota((8, 128), 1)
    b = lane // 8 % 8
    low = [get(c, 0, z)[0:2] for c in range(3) for z in range(2)]
    high = [get(c, 1, z)[6:8] for c in range(3) for z in range(2)]
    fill = jnp.zeros((4, 128), F32)
    x_lo = pltpu.roll(jnp.concatenate(low + [fill], axis=0), 64, 1)
    x_hi = pltpu.roll(jnp.concatenate(high + [fill], axis=0), 64, 1)
    y_lo, y_hi = [], []
    for group in range(2):
        lo = hi = None
        for i in range(6):
            v = get(*CXZ[group * 6 + i])
            here = b == i
            to_lo = v if i == 0 else pltpu.roll(v, 8 * i, 1)
            to_hi = pltpu.roll(v, (8 * i + 72) % 128, 1)
            lo = to_lo if lo is None else jnp.where(here, to_lo, lo)
            hi = to_hi if hi is None else jnp.where(here, to_hi, hi)
        y_lo.append(pltpu.roll(lo, 1, 0))
        y_hi.append(pltpu.roll(hi, 7, 0))
    return x_lo, x_hi, jnp.concatenate(y_lo, axis=0), jnp.concatenate(y_hi, axis=0)


def received_faces(odd_d, odd_c, drift_odd, drift_even, cross_odd, cross_even):
    m = face_masks()
    from_hi_x = jnp.where(odd_d, drift_odd, drift_even)
    from_lo_x = jnp.where(odd_d, drift_even, drift_odd)
    from_hi_y = jnp.where(odd_c, cross_odd, cross_even)
    from_lo_y = jnp.where(odd_c, cross_even, cross_odd)
    hi_y = [pltpu.roll(from_hi_y[8 * g : 8 * g + 8], 56, 1) for g in range(2)]
    lo_y = [from_lo_y[8 * g : 8 * g + 8] for g in range(2)]

    def at(c, x, z):
        r = 2 * (c * 2 + z)
        rows = (from_hi_x if x == 1 else from_lo_x)[r : r + 2]
        out = jnp.concatenate([rows] * 4, axis=0) * (m["x_hi"] if x == 1 else m["x_lo"])
        index = (c * 2 + x) * 2 + z
        g, i = index // 6, index % 6
        back = (128 - 8 * i) % 128
        hi = pltpu.roll(hi_y[g], back, 1) if back else hi_y[g]
        lo = pltpu.roll(lo_y[g], back, 1) if back else lo_y[g]
        return out + hi * m["y_hi"] + lo * m["y_lo"]

    return at


def local_step(get, tab, lane_op):
    m = face_masks()
    whole = jnp.concatenate([get(*i) for i in CXZ], axis=0)
    hi, lo = split(whole)
    product = jnp.dot(jnp.concatenate([hi, lo], axis=1), lane_op[...], preferred_element_type=F32)
    product = product[:, 0:128] + product[:, 128:256]
    turned = {}
    for i in CXZ:
        v = get(*i)
        w = pltpu.roll(v, 64, 1)
        turned[i] = (
            [v] + [pltpu.roll(v, 2 * s, 0) for s in range(1, 4)],
            [w] + [pltpu.roll(w, 2 * s, 0) for s in range(1, 4)],
        )
    out = {}
    for n, (c, x, z) in enumerate(CXZ):
        v = turned[c, x, z][0][0]
        total = product[8 * n : 8 * n + 8]
        for kind in range(2):
            for s in range(4):
                r = (kind * 4 + s) * 8
                total = total + turned[c, x, z][kind][s] * tab[r : r + 8, :]
        beside = turned[c, 1 - x, z][1]
        total = total + (beside[3] * m["x_hi"] if x == 0 else beside[1] * m["x_lo"])
        total = total + pltpu.roll(pltpu.roll(v, 56, 1), 7, 0) * m["y_in_hi"]
        total = total + pltpu.roll(pltpu.roll(v, 72, 1), 1, 0) * m["y_in_lo"]
        across = turned[c, x, 1 - z][0][0]
        if z == 0:
            total = total + pltpu.roll(across, 7, 1) * m["z_hi"]
        else:
            total = total + pltpu.roll(across, 121, 1) * m["z_lo"]
        out[c, x, z] = total
    return out


def field_operand(get):
    lane = iota((96, 128), 1)
    whole = jnp.concatenate([get(*i) for i in CXZ], axis=0)
    hi = whole.astype(BF16).astype(F32)
    lo = whole - hi
    first = jnp.where(lane < 64, hi, pltpu.roll(lo, 64, 1)).astype(BF16)
    second = jnp.where(lane < 64, pltpu.roll(hi, 64, 1), lo).astype(BF16)
    rows = jnp.concatenate([first, second], axis=0)
    return jnp.concatenate([rows, rows], axis=1)


def couple(n_tiles, coords_at, velocity_at, drag_at, host_at, field, emit, base, wts, ra, group=4):
    even = node_tables([0, 0, 2, 2, 4, 4, 6, 6])
    odd = node_tables([1, 1, 3, 3, 5, 5, 7, 7])
    plain = node_tables(list(range(8)))
    y_sub = iota((8, 128), 0) % 2
    total = None
    for g in range(n_tiles // group):
        for t in range(g * group, g * group + group):
            cols = slice(128 * t, 128 * t + 128)
            sx, sy, sz = coords_at(t)
            y_of = (host_at(t) // 2) % 2
            keep = y_of == y_sub
            base[0:8, cols] = jnp.where(keep, lagrange(sx, even), 0.0)
            base[8:16, cols] = jnp.where(keep, lagrange(sx, odd), 0.0)
            lb, lc = lagrange(sy, plain), lagrange(sz, plain)
            w = jnp.concatenate([jnp.broadcast_to(lb[b : b + 1], (8, 128)) * lc for b in range(8)], axis=0)
            hi, lo = split(w)
            wts[0:64, cols] = hi
            wts[64:128, cols] = hi
            wts[128:192, cols] = lo
            wts[192:256, cols] = lo
        span = slice(128 * g * group, 128 * (g + 1) * group)
        h = jnp.dot(field, wts[:, span], preferred_element_type=F32)
        for t in range(g * group, g * group + group):
            cols = slice(128 * t, 128 * t + 128)
            sub = slice(128 * (t - g * group), 128 * (t - g * group) + 128)
            code = host_at(t)
            q = (code // 4) * 2 + code % 2
            drag = drag_at(t) * (-MASS)
            at = [q == i for i in range(4)]
            lines = [base[0:8, cols], base[8:16, cols]]
            carried = []
            for c in range(3):
                acc = None
                for a1 in range(2):
                    r = (a1 * 12 + c * 4) * 8
                    v = h[r : r + 8, sub]
                    for i in range(1, 4):
                        v = jnp.where(at[i], h[r + 8 * i : r + 8 * i + 8, sub], v)
                    v = v * lines[a1]
                    acc = v if acc is None else acc + v
                carried.append(jnp.sum(acc, axis=0, keepdims=True))
            emit(t, carried)
            speed = velocity_at(t)
            for c in range(3):
                r = drag * (carried[c] - speed[c])
                for a1 in range(2):
                    v = r * lines[a1]
                    hi = v.astype(BF16).astype(F32)
                    lo = v - hi
                    for part, value in enumerate((hi, lo)):
                        first = ((part * 2 + a1) * 3 + c) * 32
                        rows = jnp.concatenate([jnp.where(at[i], value, 0.0) for i in range(4)], axis=0)
                        ra[first : first + 32, cols] = rows.astype(BF16)
        d = lax.dot_general(
            ra[:, span], wts[64:192, span], (((1,), (1,)), ((), ())), preferred_element_type=F32
        )
        total = d if total is None else total + d
    d = total[0:192] + total[192:384]
    d = d + pltpu.roll(d, 64, 1)
    return jnp.where(iota((96, 128), 1) < 64, d[0:96], d[96:192])


def lists_onehot(mig, store):
    high = []
    lane_row = iota((128, 128), 0)
    for t in range(16):
        idx = mig[t : t + 1, :]
        store[:, 128 * t : 128 * t + 128] = jnp.where(lane_row == (idx & 127), 1.0, 0.0).astype(BF16)
        high.append(idx >> 7)
    return high


def send_kernel(fl, co, ve, dr, ho, mi, o0, o1, o2, o3, vf, vc, vv, vd, vh, vm, table, onehot, sems):
    copies = [
        pltpu.make_async_copy(src, dst, sems.at[n])
        for n, (src, dst) in enumerate(((mi, vm), (co, vc), (ve, vv), (dr, vd), (ho, vh), (fl, vf)))
    ]
    for copy in copies:
        copy.start()
    copies[0].wait()
    high = lists_onehot(vm, onehot)
    for copy in copies[1:]:
        copy.wait()
    for c in range(3):
        table[pl.ds(c, 16, stride=8), :] = vc[16 * c : 16 * c + 16, :]
        table[pl.ds(3 + c, 16, stride=8), :] = vv[16 * c : 16 * c + 16, :]
    table[pl.ds(6, 16, stride=8), :] = vd[...]
    table[pl.ds(7, 16, stride=8), :] = vh[...].astype(F32)
    hi, lo = split(table[...])
    hi_lo = jnp.concatenate([hi, lo], axis=1)
    odd_d, odd_c = parity("drift"), parity("cross")
    x_lo, x_hi, y_lo, y_hi = pack_faces(functools.partial(tile_of, vf))
    o0[32:48, :] = jnp.where(odd_d, x_hi, x_lo)
    o1[32:48, :] = jnp.where(odd_d, x_lo, x_hi)
    o2[32:48, :] = jnp.where(odd_c, y_hi, y_lo)
    o3[32:48, :] = jnp.where(odd_c, y_lo, y_hi)
    for t in range(4):
        span = onehot[:, 512 * t : 512 * t + 512]
        y = jnp.dot(hi_lo, jnp.concatenate([span, span], axis=0), preferred_element_type=F32)
        found = []
        for d in range(4):
            h = high[4 * t + d]
            g = jnp.zeros((8, 128), F32)
            for row in range(16):
                g = jnp.where(h == row, y[8 * row : 8 * row + 8, 128 * d : 128 * d + 128], g)
            found.append(g)
        rows = slice(8 * t, 8 * t + 8)
        o0[rows, :] = jnp.where(odd_d, found[1], found[0])
        o1[rows, :] = jnp.where(odd_d, found[0], found[1])
        o2[rows, :] = jnp.where(odd_c, found[3], found[2])
        o3[rows, :] = jnp.where(odd_c, found[2], found[3])


def own_kernel(fl, co, ve, dr, ho, mi, tab, lane_op, dep_out, vel_out, base_out, operand_out, onehot, car, base, wts, ra):
    high = lists_onehot(mi, onehot)
    sub16 = iota((16, 128), 0)
    rows = jnp.concatenate([jnp.where(h == sub16, 1.0, 0.0) for h in high], axis=1).astype(BF16)
    listed = lax.dot_general(rows, onehot[...], (((1,), (1,)), ((), ())), preferred_element_type=F32)
    own = jnp.where(listed > 0.5, 0.0, 1.0)
    get = functools.partial(tile_of, fl)
    field = field_operand(get)
    operand_out[...] = field
    drag_own = dr[...] * own

    def emit(t, carried):
        for c in range(3):
            car[16 * c + t : 16 * c + t + 1, :] = carried[c]

    dep_out[...] = couple(
        16,
        lambda t: [row_of(co, 16 * c + t) for c in range(3)],
        lambda t: [row_of(ve, 16 * c + t) for c in range(3)],
        lambda t: jnp.broadcast_to(drag_own[t : t + 1], (8, 128)),
        lambda t: row_of(ho, t),
        field, emit, base, wts, ra,
    )
    for c in range(3):
        r = slice(16 * c, 16 * c + 16)
        vel_out[r, :] = ve[r, :] + dr[...] * (car[r, :] * own - ve[r, :])
    out = local_step(get, tab, lane_op)
    for n, i in enumerate(CXZ):
        base_out[8 * n : 8 * n + 8, :] = out[i]


def host_kernel(r0, r1, r2, r3, operand, dep_in, base_in, u_out, dep_out, o0, o1, o2, o3, base, wts, ra):
    received, sent = (r0, r1, r2, r3), (o0, o1, o2, o3)
    odd_d, odd_c = parity("drift"), parity("cross")
    pick = lambda t, v: row_of(received[t // 4], 8 * (t % 4) + v)

    def emit(t, carried):
        for c in range(3):
            sent[t // 4][4 * (t % 4) + c : 4 * (t % 4) + c + 1, :] = carried[c]
        sent[t // 4][4 * (t % 4) + 3 : 4 * (t % 4) + 4, :] = carried[0]

    dep = dep_in[...] + couple(
        16,
        lambda t: [pick(t, c) for c in range(3)],
        lambda t: [pick(t, 3 + c) for c in range(3)],
        lambda t: pick(t, 6),
        lambda t: pick(t, 7).astype(jnp.int32),
        operand[...], emit, base, wts, ra,
    )
    dep_out[...] = dep
    faces = received_faces(odd_d, odd_c, *[r[32:48, :] for r in received])
    new = {}
    for n, i in enumerate(CXZ):
        r = slice(8 * n, 8 * n + 8)
        new[i] = base_in[r, :] + faces(*i) + 0.5 * dep[r]
        u_out[r, :] = new[i]
    x_lo, x_hi, y_lo, y_hi = pack_faces(lambda c, x, z: new[c, x, z])
    o0[16:32, :] = jnp.where(odd_d, x_hi, x_lo)
    o1[16:32, :] = jnp.where(odd_d, x_lo, x_hi)
    o2[16:32, :] = jnp.where(odd_c, y_hi, y_lo)
    o3[16:32, :] = jnp.where(odd_c, y_lo, y_hi)


def second_kernel(u, dep, tab, lane_op, out_ref):
    out = local_step(functools.partial(tile_of, u), tab, lane_op)
    for n, i in enumerate(CXZ):
        r = slice(8 * n, 8 * n + 8)
        out_ref[r, :] = out[i] + 0.5 * dep[r, :]


def last_kernel(r0, r1, r2, r3, base, vel, dr, mi, onehot, fluid_out, vel_out):
    odd_d, odd_c = parity("drift"), parity("cross")
    faces = received_faces(odd_d, odd_c, *[r[16:32, :] for r in (r0, r1, r2, r3)])
    for n, i in enumerate(CXZ):
        r = slice(8 * n, 8 * n + 8)
        fluid_out[r, :] = base[r, :] + faces(*i)
    sub16 = iota((16, 128), 0)
    columns = []
    for t in range(4):
        rows = slice(4 * t, 4 * t + 4)
        back = [
            jnp.where(odd_d, r1[rows, :], r0[rows, :]),
            jnp.where(odd_d, r0[rows, :], r1[rows, :]),
            jnp.where(odd_c, r3[rows, :], r2[rows, :]),
            jnp.where(odd_c, r2[rows, :], r3[rows, :]),
        ]
        for d in range(4):
            at = (mi[4 * t + d : 4 * t + d + 1, :] >> 7) == sub16
            columns.append(jnp.concatenate([jnp.where(at, back[d][c : c + 1], 0.0) for c in range(3)], axis=0))
    hi, lo = split(jnp.concatenate(columns, axis=1))
    put = lax.dot_general(
        jnp.concatenate([hi, lo], axis=0), onehot[...], (((1,), (1,)), ((), ())), preferred_element_type=F32
    )
    put = put[0:48] + put[48:96]
    for c in range(3):
        r = slice(16 * c, 16 * c + 16)
        vel_out[r, :] = vel[r, :] + dr[...] * put[r]


def shape(rows, dtype=F32, lanes=128):
    return jax.ShapeDtypeStruct((rows, lanes), dtype)


def call(kernel, outs, scratch=(), in_specs=None, cost=0, **kw):
    if in_specs is not None:
        kw["in_specs"] = in_specs
    return pl.pallas_call(
        kernel,
        out_shape=outs,
        scratch_shapes=list(scratch),
        cost_estimate=pl.CostEstimate(flops=cost, bytes_accessed=0, transcendentals=0),
        compiler_params=pltpu.CompilerParams(vmem_limit_bytes=VMEM),
        **kw,
    )


def swap(block, axis, odd):
    count = lax.axis_size(axis)
    pairs = []
    for i in range(odd, count + odd, 2):
        first, other = i % count, (i + 1) % count
        pairs += [(first, other), (other, first)]
    return lax.ppermute(block, axis, pairs)


def exchange(blocks):
    order = (("drift", 1), ("drift", 0), ("cross", 1), ("cross", 0))
    return [swap(block, axis, odd) for block, (axis, odd) in zip(blocks, order)]


def per_device(fluid_field, coords, velocity, drag_factor, host_ids, migrants):
    field = fluid_field.reshape(3, 2, 2, 8, 128).transpose(0, 1, 3, 2, 4).reshape(96, 128)
    args = (
        field,
        coords.reshape(48, 128),
        velocity.reshape(48, 128),
        drag_factor.reshape(16, 128),
        host_ids.reshape(16, 128),
        migrants.reshape(4, 4, 128).transpose(1, 0, 2).reshape(16, 128),
    )
    tab, lane_op = (jnp.asarray(t) for t in operator_tables())
    couple_scratch = [pltpu.VMEM((16, 2048), F32), pltpu.VMEM((256, 2048), BF16), pltpu.VMEM((384, 2048), BF16)]
    sends = call(
        send_kernel,
        [shape(48)] * 4,
        [pltpu.VMEM(a.shape, a.dtype) for a in args]
        + [pltpu.VMEM((128, 128), F32), pltpu.VMEM((128, 2048), BF16), pltpu.SemaphoreType.DMA((6,))],
        in_specs=[pl.BlockSpec(memory_space=pl.ANY)] * 6,
    )(*args)
    received = exchange(sends)
    dep, vel, base, operand, onehot = call(
        own_kernel,
        [shape(96), shape(48), shape(96), shape(192, BF16, 256), shape(128, BF16, 2048)],
        [pltpu.VMEM((48, 128), F32)] + couple_scratch,
        cost=1 << 31,
    )(*args, tab, lane_op)
    u, dep, *sends = call(host_kernel, [shape(96)] * 2 + [shape(32)] * 4, couple_scratch)(
        *received, operand, dep, base
    )
    received = exchange(sends)
    base = call(second_kernel, shape(96), cost=1 << 30)(u, dep, tab, lane_op)
    fluid, vel = call(last_kernel, [shape(96), shape(48)])(*received, base, vel, args[3], args[5], onehot)
    fluid = fluid.reshape(3, 2, 8, 2, 128).transpose(0, 1, 3, 2, 4).reshape(3, 2, 2, 1024)
    return fluid, vel.reshape(3, 1, 1, 2048)


def solution(mesh):
    field = P(None, "drift", "cross", None)
    scalar = P("drift", "cross", None)
    return jax.shard_map(
        per_device,
        mesh=mesh,
        in_specs=(field, field, field, scalar, scalar, P("drift", "cross", None, None)),
        out_specs=(field, field),
        check_vma=False,
    )
```

time: 495 us -> 27.7 us (0.06); the launches traced: 488 us -> 27.3 us
  other arithmetic: 233 us -> 0 us
  loops' own time: 141 us -> 0 us
  local copies, waits for them, and re-layouts: 66.3 us -> 5.27 us
  starting transfers between devices: 31.4 us -> 13.6 us
  matrix products: 12.9 us -> 0 us
  Pallas kernels: 0 us -> 5.5 us
    scatter-add x4 -> x0, other arithmetic: 172 us -> none  [the longest x2 172 us: visit(): return (deposit.at[:, safe_rows, :].add(spread), updated)]
    another operation x1 -> x0, loops' own time: 141 us -> none  [scan_rows(): deposit, updated = lax.scan(visit, start, pieces)]
    gather x2 -> x0, local copies, waits for them, and re-layouts: 26.5 us -> none  [couple_rows(): sampled = element_table[:, safe_rows, :]]
    div x6 -> x0, other arithmetic: 25.3 us -> none  [lagrange_rows(): rows_out.append(numerator / denominator)]
    ppermute x16 -> x8, starting transfers between devices: 31.4 us -> 13.6 us  [swap(): return lax.ppermute(block, axis, pairs)]
    add x2 -> x0, local copies, waits for them, and re-layouts: 13.5 us -> none  [the longest x1 13.5 us: operator_transposed(): jnp.kron(jnp.kron(second, ident), ident)]
    dot_general x11 -> x0, matrix products: 12.9 us -> none  [the longest x2 4.64 us: per_device(): jnp.dot(field_state, operator_t, precision=highest)]
    mul x8 -> x0, other arithmetic: 12.2 us -> none  [the longest x2 8.62 us: couple_rows(): spread = reaction[:, :, None] * weights[None]]
  transfers between devices with their start and end apart: 16 -> 8, of which waited for: 6 -> 1; matrix products, arithmetic and copies ran while one was open for 9% -> 0% of each run, Pallas kernels for 0% -> 8%
where the time goes in v1:
time: 27.7 us; the launch traced here: 27.3 us
  starting transfers between devices  13.6 us (49%)
  Pallas kernels  5.5 us (20%)
  local copies, waits for them, and re-layouts  5.27 us (19%)
  waiting for transfers between devices  2.23 us (8%)
  between operations  0.73 us (3%)
    ppermute x8, starting transfers between devices, swap(): return lax.ppermute(block, axis, pairs)  13.6 us
    unnamed x20, local copies, waits for them, and re-layouts  5.27 us
    ppermute x8, waiting for transfers between devices, swap(): return lax.ppermute(block, axis, pairs)  2.23 us
    pallas_call x1, Pallas kernels, per_device(): call(own_kernel, [shape(96), shape(48), shape(96), shape(192, BF16, 256),...  1.88 us
    pallas_call x1, Pallas kernels, per_device(): call(host_kernel, [shape(96)] * 2 + [shape(32)] * 4, couple_scratch)  1.83 us
    pallas_call x1, Pallas kernels, per_device(): call(last_kernel, [shape(96), shape(48)])  0.92 us
    pallas_call x1, Pallas kernels, per_device(): call(send_kernel, [shape(48)] * 4, [pltpu.VMEM(a.shape, a.dtype) for a in...  0.69 us
  transfers between devices with their start and end apart: 8, of which 1 were waited for; matrix products, arithmetic and copies ran while one was open for 0% of the time, Pallas kernels for 8%

profile of v1, /device:TPU:1, one launch (start us, length us, event | category | flops | bytes accessed | tf_op | source)
XLA Modules:
  0.0 27.3 jit_solution(14623650076890653356)
XLA Ops:
  0.6 0.0 copy-start.1
  0.6 0.7 %copy-done.1 = f32[1,1,2048]{2,1,0:T(1,128)S(1)} copy-done((f32[1,1,2048]{2,1,0:T(1,128)S(1)}, f32[1,1,2048]{2,1,0:T(1,128)}, u32[]{:S(2)}) %copy-start.1) | copy-done | bytes 8216
  1.3 0.0 copy-start
  1.3 0.8 %copy-done = f32[3,2,2,1024]{3,2,1,0:T(2,128)S(1)} copy-done((f32[3,2,2,1024]{3,2,1,0:T(2,128)S(1)}, f32[3,2,2,1024]{3,2,1,0:T(2,128)}, u32[]{:S(2)}) %copy-start) | copy-done | bytes 49176
  2.1 0.0 copy-start.2
  2.1 0.7 %copy-done.2 = s32[1,1,4,512]{3,2,1,0:T(4,128)S(1)} copy-done((s32[1,1,4,512]{3,2,1,0:T(4,128)S(1)}, s32[1,1,4,512]{3,2,1,0:T(4,128)}, u32[]{:S(2)}) %copy-start.2) | copy-done | bytes 8216
  2.8 0.0 copy-start.4
  2.8 0.7 %copy-done.4 = f32[3,1,1,2048]{3,2,1,0:T(1,128)S(1)} copy-done((f32[3,1,1,2048]{3,2,1,0:T(1,128)S(1)}, f32[3,1,1,2048]{3,2,1,0:T(1,128)}, u32[]{:S(2)}) %copy-start.4) | copy-done | bytes 24600
  3.6 0.0 copy-start.5
  3.6 0.7 %copy-done.5 = f32[3,1,1,2048]{3,2,1,0:T(1,128)S(1)} copy-done((f32[3,1,1,2048]{3,2,1,0:T(1,128)S(1)}, f32[3,1,1,2048]{3,2,1,0:T(1,128)}, u32[]{:S(2)}) %copy-start.5) | copy-done | bytes 24600
  4.3 0.0 copy-start.6
  4.3 0.7 %copy-done.6 = s32[1,1,2048]{2,1,0:T(1,128)S(1)} copy-done((s32[1,1,2048]{2,1,0:T(1,128)S(1)}, s32[1,1,2048]{2,1,0:T(1,128)}, u32[]{:S(2)}) %copy-start.6) | copy-done | bytes 8216
  5.0 0.0 copy-start.9
  5.0 0.7 %shard_map.95 = (f32[48,128]{1,0:T(8,128)S(1)}, f32[48,128]{1,0:T(8,128)S(1)}, f32[48,128]{1,0:T(8,128)S(1)}, f32[48,128]{1,0:T(8,128)S(1)}) custom-call(f32[96,128]{1,0:T(8,128)S(1)} %bitcast.20, f32[48,128]{1,0:T(8,128)S(1)} %bitcast.28, f32[48,128]{1,0:T(8,128)S(1)} %bitcast.30, f32[16,128]{1,0:T(8,128)S(1)} %bitcast.22, s32[16,128]{1,0:T(8,128)S(1)} %bitcast.32, ...), custom_call_target="tpu_custom_call" | custom-call | tf_op jit(solution)/shard_map/pallas_call | solution.py:470
  5.7 7.1 %collective-permute-start = (f32[48,128]{1,0:T(8,128)S(1)}, f32[48,128]{1,0:T(8,128)S(1)}, u32[]{:S(2)}, u32[]{:S(2)}) collective-permute-start(f32[48,128]{1,0:T(8,128)S(1)} %get-tuple-element.19), channel_id=1, source_target_pairs={{8,16},{16,8},{24,32},{32,24},{40,48},{48,40},{56,64},{64,56},{72,... | collective-permute-start | bytes 73736 | tf_op jit(solution)/shard_map/ppermute | solution.py:450
  12.8 0.0 collective-permute-start.1
  12.8 2.1 %collective-permute-start.2 = (f32[48,128]{1,0:T(8,128)S(1)}, f32[48,128]{1,0:T(8,128)S(1)}, u32[]{:S(2)}, u32[]{:S(2)}) collective-permute-start(f32[48,128]{1,0:T(8,128)S(1)} %get-tuple-element.21), channel_id=1, source_target_pairs={{1,2},{2,1},{3,4},{4,3},{5,6},{6,5},{7,0},{0,7},{9,10},{10,9},{11,... | collective-permute-start | bytes 73736 | tf_op jit(solution)/shard_map/ppermute | solution.py:450
  14.9 0.8 %collective-permute-start.3 = (f32[48,128]{1,0:T(8,128)S(1)}, f32[48,128]{1,0:T(8,128)S(1)}, u32[]{:S(2)}, u32[]{:S(2)}) collective-permute-start(f32[48,128]{1,0:T(8,128)S(1)} %get-tuple-element.22), channel_id=1, source_target_pairs={{0,1},{1,0},{2,3},{3,2},{4,5},{5,4},{6,7},{7,6},{8,9},{9,8},{10,11... | collective-permute-start | bytes 73736 | tf_op jit(solution)/shard_map/ppermute | solution.py:450
  15.7 0.0 copy-done.9
  15.7 0.0 copy-start.7
  15.7 0.9 %copy-done.7 = bf16[256,256]{1,0:T(8,128)(2,1)S(1)} copy-done((bf16[256,256]{1,0:T(8,128)(2,1)S(1)}, bf16[256,256]{1,0:T(8,128)(2,1)}, u32[]{:S(2)}) %copy-start.7) | copy-done | bytes 131096
  16.6 1.9 %shard_map.96 = (f32[96,128]{1,0:T(8,128)S(1)}, f32[48,128]{1,0:T(8,128)S(1)}, f32[96,128]{1,0:T(8,128)S(1)}, bf16[192,256]{1,0:T(8,128)(2,1)S(1)}, bf16[128,2048]{1,0:T(8,128)(2,1)S(1)}) custom-call(f32[96,128]{1,0:T(8,128)S(1)} %bitcast.21, f32[48,128]{1,0:T(8,128)S(1)} %bitcast.29, f32[48,128]{1,0:T(8,128)S(1)} %bitcast.31, f32[16,128]{1,0:T(8,128)S(1)} %bitcast.23, ...), custom_call_target="tpu_custom_call" | custom-call | flops 2147483648 | tf_op jit(solution)/shard_map/pallas_call | solution.py:478
  18.5 0.0 collective-permute-done.r0
  18.5 0.0 collective-permute-done.1.r1
  18.5 0.0 collective-permute-done.2.r2
  18.5 0.0 collective-permute-done.3.r3
  18.5 0.0 copy-start.8
  18.5 1.8 %shard_map.97 = (f32[96,128]{1,0:T(8,128)S(1)}, f32[96,128]{1,0:T(8,128)S(1)}, f32[32,128]{1,0:T(8,128)S(1)}, f32[32,128]{1,0:T(8,128)S(1)}, f32[32,128]{1,0:T(8,128)S(1)}, /*index=5*/f32[32,128]{1,0:T(8,128)S(1)}) custom-call(f32[48,128]{1,0:T(8,128)S(1)} %collective-permute-done.r0, f32[48,128]{1,0:T(8,128)S(1)} %collective-permute-done.1.r1, ...), custom_call_target="tpu_custom_call" | custom-call | tf_op jit(solution)/shard_map/pallas_call | solution.py:484
  20.4 0.7 %collective-permute-start.4 = (f32[32,128]{1,0:T(8,128)S(1)}, f32[32,128]{1,0:T(8,128)S(1)}, u32[]{:S(2)}, u32[]{:S(2)}) collective-permute-start(f32[32,128]{1,0:T(8,128)S(1)} %get-tuple-element.26), channel_id=1, source_target_pairs={{8,16},{16,8},{24,32},{32,24},{40,48},{48,40},{56,64},{64,56},{72,... | collective-permute-start | bytes 49160 | tf_op jit(solution)/shard_map/ppermute | solution.py:450
  21.1 0.9 %collective-permute-start.5 = (f32[32,128]{1,0:T(8,128)S(1)}, f32[32,128]{1,0:T(8,128)S(1)}, u32[]{:S(2)}, u32[]{:S(2)}) collective-permute-start(f32[32,128]{1,0:T(8,128)S(1)} %get-tuple-element.27), channel_id=1, source_target_pairs={{0,8},{8,0},{16,24},{24,16},{32,40},{40,32},{48,56},{56,48},{64,72... | collective-permute-start | bytes 49160 | tf_op jit(solution)/shard_map/ppermute | solution.py:450
  22.0 1.9 %collective-permute-start.6 = (f32[32,128]{1,0:T(8,128)S(1)}, f32[32,128]{1,0:T(8,128)S(1)}, u32[]{:S(2)}, u32[]{:S(2)}) collective-permute-start(f32[32,128]{1,0:T(8,128)S(1)} %get-tuple-element.28), channel_id=1, source_target_pairs={{1,2},{2,1},{3,4},{4,3},{5,6},{6,5},{7,0},{0,7},{9,10},{10,9},{11,... | collective-permute-start | bytes 49160 | tf_op jit(solution)/shard_map/ppermute | solution.py:450
  24.0 0.0 collective-permute-start.7
  24.0 0.0 copy-done.8
  24.0 0.0 copy-start.3
  24.0 0.2 shard_map.98.base
  24.2 2.2 %collective-permute-done.4.r0 = f32[32,128]{1,0:T(8,128)S(1)} collective-permute-done((f32[32,128]{1,0:T(8,128)S(1)}, f32[32,128]{1,0:T(8,128)S(1)}, u32[]{:S(2)}, u32[]{:S(2)}) %collective-permute-start.4) | collective-permute-done | bytes 16416 | tf_op jit(solution)/shard_map/ppermute | solution.py:450
  26.4 0.0 collective-permute-done.5.r1
  26.4 0.0 collective-permute-done.6.r2
  26.4 0.0 collective-permute-done.7.r3
  26.4 0.0 copy-done.3
  26.4 0.9 %shard_map.99 = (f32[96,128]{1,0:T(8,128)}, f32[48,128]{1,0:T(8,128)}) custom-call(f32[32,128]{1,0:T(8,128)S(1)} %collective-permute-done.4.r0, f32[32,128]{1,0:T(8,128)S(1)} %collective-permute-done.5.r1, f32[32,128]{1,0:T(8,128)S(1)} %collective-permute-done.6.r2, f32[32,128]{1,0:T(8,128)S(1)} %collective-permute-done.7.r3, f32[96,128]{1,0:T(8,128)S(1)} %shard_map.98.base, ...), custom_call_target="tpu_custom_call" | custom-call | tf_op jit(solution)/shard_map/pallas_call | solution.py:489
Async XLA Ops:
  0.6 0.7 %copy-start.1 = (f32[1,1,2048]{2,1,0:T(1,128)S(1)}, f32[1,1,2048]{2,1,0:T(1,128)}, u32[]{:S(2)}) copy-start(f32[1,1,2048]{2,1,0:T(1,128)} %param.11) | copy-start | bytes 24580
  1.3 0.8 %copy-start = (f32[3,2,2,1024]{3,2,1,0:T(2,128)S(1)}, f32[3,2,2,1024]{3,2,1,0:T(2,128)}, u32[]{:S(2)}) copy-start(f32[3,2,2,1024]{3,2,1,0:T(2,128)} %param.8) | copy-start | bytes 147460
  2.1 0.7 %copy-start.2 = (s32[1,1,4,512]{3,2,1,0:T(4,128)S(1)}, s32[1,1,4,512]{3,2,1,0:T(4,128)}, u32[]{:S(2)}) copy-start(s32[1,1,4,512]{3,2,1,0:T(4,128)} %param.13) | copy-start | bytes 24580
  2.8 0.7 %copy-start.4 = (f32[3,1,1,2048]{3,2,1,0:T(1,128)S(1)}, f32[3,1,1,2048]{3,2,1,0:T(1,128)}, u32[]{:S(2)}) copy-start(f32[3,1,1,2048]{3,2,1,0:T(1,128)} %param.9) | copy-start | bytes 73732
  3.6 0.7 %copy-start.5 = (f32[3,1,1,2048]{3,2,1,0:T(1,128)S(1)}, f32[3,1,1,2048]{3,2,1,0:T(1,128)}, u32[]{:S(2)}) copy-start(f32[3,1,1,2048]{3,2,1,0:T(1,128)} %param.10) | copy-start | bytes 73732
  4.3 0.7 %copy-start.6 = (s32[1,1,2048]{2,1,0:T(1,128)S(1)}, s32[1,1,2048]{2,1,0:T(1,128)}, u32[]{:S(2)}) copy-start(s32[1,1,2048]{2,1,0:T(1,128)} %param.12) | copy-start | bytes 24580
  5.0 10.7 %copy-start.9 = (f32[64,128]{1,0:T(8,128)S(1)}, f32[64,128]{1,0:T(8,128)}, u32[]{:S(2)}) copy-start(f32[64,128]{1,0:T(8,128)} %constant.4.clone.tab) | copy-start | bytes 98308
  5.7 12.8 %collective-permute-start = (f32[48,128]{1,0:T(8,128)S(1)}, f32[48,128]{1,0:T(8,128)S(1)}, u32[]{:S(2)}, u32[]{:S(2)}) collective-permute-start(f32[48,128]{1,0:T(8,128)S(1)} %get-tuple-element.19), channel_id=1, source_target_pairs={{8,16},{16,8},{24,32},{32,24},{40,48},{48,40},{56,64},{64,56},{72,... | collective-permute-start | bytes 73736 | tf_op jit(solution)/shard_map/ppermute | solution.py:450
  12.8 5.7 %collective-permute-start.1 = (f32[48,128]{1,0:T(8,128)S(1)}, f32[48,128]{1,0:T(8,128)S(1)}, u32[]{:S(2)}, u32[]{:S(2)}) collective-permute-start(f32[48,128]{1,0:T(8,128)S(1)} %get-tuple-element.20), channel_id=1, source_target_pairs={{0,8},{8,0},{16,24},{24,16},{32,40},{40,32},{48,56},{56,48},{64,72... | collective-permute-start | bytes 73736 | tf_op jit(solution)/shard_map/ppermute | solution.py:450
  12.8 5.7 %collective-permute-start.2 = (f32[48,128]{1,0:T(8,128)S(1)}, f32[48,128]{1,0:T(8,128)S(1)}, u32[]{:S(2)}, u32[]{:S(2)}) collective-permute-start(f32[48,128]{1,0:T(8,128)S(1)} %get-tuple-element.21), channel_id=1, source_target_pairs={{1,2},{2,1},{3,4},{4,3},{5,6},{6,5},{7,0},{0,7},{9,10},{10,9},{11,... | collective-permute-start | bytes 73736 | tf_op jit(solution)/shard_map/ppermute | solution.py:450
  14.9 3.6 %collective-permute-start.3 = (f32[48,128]{1,0:T(8,128)S(1)}, f32[48,128]{1,0:T(8,128)S(1)}, u32[]{:S(2)}, u32[]{:S(2)}) collective-permute-start(f32[48,128]{1,0:T(8,128)S(1)} %get-tuple-element.22), channel_id=1, source_target_pairs={{0,1},{1,0},{2,3},{3,2},{4,5},{5,4},{6,7},{7,6},{8,9},{9,8},{10,11... | collective-permute-start | bytes 73736 | tf_op jit(solution)/shard_map/ppermute | solution.py:450
  15.7 0.9 %copy-start.7 = (bf16[256,256]{1,0:T(8,128)(2,1)S(1)}, bf16[256,256]{1,0:T(8,128)(2,1)}, u32[]{:S(2)}) copy-start(bf16[256,256]{1,0:T(8,128)(2,1)} %constant.5.clone.lane_op) | copy-start | bytes 393220
  18.5 5.5 %copy-start.8 = (bf16[256,256]{1,0:T(8,128)(2,1)S(1)}, bf16[256,256]{1,0:T(8,128)(2,1)}, u32[]{:S(2)}) copy-start(bf16[256,256]{1,0:T(8,128)(2,1)} %constant.5.clone.lane_op) | copy-start | bytes 393220
  20.4 6.0 %collective-permute-start.4 = (f32[32,128]{1,0:T(8,128)S(1)}, f32[32,128]{1,0:T(8,128)S(1)}, u32[]{:S(2)}, u32[]{:S(2)}) collective-permute-start(f32[32,128]{1,0:T(8,128)S(1)} %get-tuple-element.26), channel_id=1, source_target_pairs={{8,16},{16,8},{24,32},{32,24},{40,48},{48,40},{56,64},{64,56},{72,... | collective-permute-start | bytes 49160 | tf_op jit(solution)/shard_map/ppermute | solution.py:450
  21.1 5.3 %collective-permute-start.5 = (f32[32,128]{1,0:T(8,128)S(1)}, f32[32,128]{1,0:T(8,128)S(1)}, u32[]{:S(2)}, u32[]{:S(2)}) collective-permute-start(f32[32,128]{1,0:T(8,128)S(1)} %get-tuple-element.27), channel_id=1, source_target_pairs={{0,8},{8,0},{16,24},{24,16},{32,40},{40,32},{48,56},{56,48},{64,72... | collective-permute-start | bytes 49160 | tf_op jit(solution)/shard_map/ppermute | solution.py:450
  22.0 4.4 %collective-permute-start.6 = (f32[32,128]{1,0:T(8,128)S(1)}, f32[32,128]{1,0:T(8,128)S(1)}, u32[]{:S(2)}, u32[]{:S(2)}) collective-permute-start(f32[32,128]{1,0:T(8,128)S(1)} %get-tuple-element.28), channel_id=1, source_target_pairs={{1,2},{2,1},{3,4},{4,3},{5,6},{6,5},{7,0},{0,7},{9,10},{10,9},{11,... | collective-permute-start | bytes 49160 | tf_op jit(solution)/shard_map/ppermute | solution.py:450
  24.0 2.4 %collective-permute-start.7 = (f32[32,128]{1,0:T(8,128)S(1)}, f32[32,128]{1,0:T(8,128)S(1)}, u32[]{:S(2)}, u32[]{:S(2)}) collective-permute-start(f32[32,128]{1,0:T(8,128)S(1)} %get-tuple-element.29), channel_id=1, source_target_pairs={{0,1},{1,0},{2,3},{3,2},{4,5},{5,4},{6,7},{7,6},{8,9},{9,8},{10,11... | collective-permute-start | bytes 49160 | tf_op jit(solution)/shard_map/ppermute | solution.py:450
  24.0 2.4 %copy-start.3 = (s32[1,1,4,512]{3,2,1,0:T(4,128)S(1)}, s32[1,1,4,512]{3,2,1,0:T(4,128)}, u32[]{:S(2)}) copy-start(s32[1,1,4,512]{3,2,1,0:T(4,128)} %param.13) | copy-start | bytes 24580

commit v2 on v1

--- a/solution.py
+++ b/solution.py
@@ -284,11 +284,11 @@
     return high
 
 
-def send_kernel(fl, co, ve, dr, ho, mi, o0, o1, o2, o3, vf, vc, vv, vd, vh, vm, table, onehot, sems):
-    copies = [
-        pltpu.make_async_copy(src, dst, sems.at[n])
-        for n, (src, dst) in enumerate(((mi, vm), (co, vc), (ve, vv), (dr, vd), (ho, vh), (fl, vf)))
-    ]
+def send_kernel(
+    fl, co, ve, dr, ho, mi, ta, la, o0, o1, o2, o3, vf, vc, vv, vd, vh, vm, vt, vl, onehot, table, sems
+):
+    pairs = ((mi, vm), (co, vc), (ve, vv), (dr, vd), (ho, vh), (fl, vf), (ta, vt), (la, vl))
+    copies = [pltpu.make_async_copy(src, dst, sems.at[n]) for n, (src, dst) in enumerate(pairs)]
     for copy in copies:
         copy.start()
     copies[0].wait()
@@ -325,8 +325,10 @@
         o3[rows, :] = jnp.where(odd_c, found[2], found[3])
 
 
-def own_kernel(fl, co, ve, dr, ho, mi, tab, lane_op, dep_out, vel_out, base_out, operand_out, onehot, car, base, wts, ra):
-    high = lists_onehot(mi, onehot)
+def own_kernel(
+    fl, co, ve, dr, ho, mi, tab, lane_op, onehot, dep_out, vel_out, base_out, operand_out, car, base, wts, ra
+):
+    high = [mi[t : t + 1, :] >> 7 for t in range(16)]
     sub16 = iota((16, 128), 0)
     rows = jnp.concatenate([jnp.where(h == sub16, 1.0, 0.0) for h in high], axis=1).astype(BF16)
     listed = lax.dot_general(rows, onehot[...], (((1,), (1,)), ((), ())), preferred_element_type=F32)
@@ -465,22 +467,23 @@
         host_ids.reshape(16, 128),
         migrants.reshape(4, 4, 128).transpose(1, 0, 2).reshape(16, 128),
     )
-    tab, lane_op = (jnp.asarray(t) for t in operator_tables())
     couple_scratch = [pltpu.VMEM((16, 2048), F32), pltpu.VMEM((256, 2048), BF16), pltpu.VMEM((384, 2048), BF16)]
-    sends = call(
+    args += tuple(jnp.asarray(t) for t in operator_tables())
+    outs = call(
         send_kernel,
-        [shape(48)] * 4,
-        [pltpu.VMEM(a.shape, a.dtype) for a in args]
-        + [pltpu.VMEM((128, 128), F32), pltpu.VMEM((128, 2048), BF16), pltpu.SemaphoreType.DMA((6,))],
-        in_specs=[pl.BlockSpec(memory_space=pl.ANY)] * 6,
-    )(*args)
+        [shape(48)] * 4 + [shape(*a.shape[:1], a.dtype, a.shape[1]) for a in args] + [shape(128, BF16, 2048)],
+        [pltpu.VMEM((128, 128), F32), pltpu.SemaphoreType.DMA((8,))],
+        in_specs=[pl.BlockSpec(memory_space=pl.ANY)] * 8,
+    )(*(pltpu.with_memory_space_constraint(a, pltpu.HBM) for a in args))
+    sends, args, onehot = outs[:4], outs[4:12], outs[12]
+    tab, lane_op = args[6:]
     received = exchange(sends)
-    dep, vel, base, operand, onehot = call(
+    dep, vel, base, operand = call(
         own_kernel,
-        [shape(96), shape(48), shape(96), shape(192, BF16, 256), shape(128, BF16, 2048)],
+        [shape(96), shape(48), shape(96), shape(192, BF16, 256)],
         [pltpu.VMEM((48, 128), F32)] + couple_scratch,
         cost=1 << 31,
-    )(*args, tab, lane_op)
+    )(*args, onehot)
     u, dep, *sends = call(host_kernel, [shape(96)] * 2 + [shape(32)] * 4, couple_scratch)(
         *received, operand, dep, base
     )

time: 27.7 us -> 23.6 us (0.85)
  the two profiles are of different devices: /device:TPU:1 before, /device:TPU:8 now
where the time goes in v2:
time: 23.6 us; the launch traced here: 23.5 us
  starting transfers between devices  13 us (55%)
  Pallas kernels  6.1 us (26%)
  waiting for transfers between devices  3.67 us (16%)
  between operations  0.71 us (3%)
    ppermute x8, starting transfers between devices, swap(): return lax.ppermute(block, axis, pairs)  13 us
    ppermute x8, waiting for transfers between devices, swap(): return lax.ppermute(block, axis, pairs)  3.67 us
    pallas_call x1, Pallas kernels, per_device(): call(host_kernel, [shape(96)] * 2 + [shape(32)] * 4, couple_scratch)  1.83 us
    pallas_call x1, Pallas kernels, per_device(): call(own_kernel, [shape(96), shape(48), shape(96), shape(192, BF16, 256)]...  1.71 us
    pallas_call x1, Pallas kernels, per_device(): call(send_kernel, [shape(48)] * 4 + [shape(*a.shape[:1], a.dtype, a.shape...  1.47 us
    pallas_call x1, Pallas kernels, per_device(): call(last_kernel, [shape(96), shape(48)])  0.92 us
  transfers between devices with their start and end apart: 8, of which 2 were waited for; matrix products, arithmetic and copies ran while one was open for 0% of the time, Pallas kernels for 8%

profile of v2, /device:TPU:8, one launch (start us, length us, event | category | flops | bytes accessed | tf_op | source)
XLA Modules:
  0.0 23.5 jit_solution(16148947069772401906)
XLA Ops:
  0.6 1.5 %shard_map.95 = (f32[48,128]{1,0:T(8,128)S(1)}, f32[48,128]{1,0:T(8,128)S(1)}, f32[48,128]{1,0:T(8,128)S(1)}, f32[48,128]{1,0:T(8,128)S(1)}, f32[96,128]{1,0:T(8...) custom-call(f32[96,128]{1,0:T(8,128)} %bitcast.20, ...), custom_call_target="tpu_custom_call" | custom-call | tf_op jit(solution)/shard_map/pallas_call | solution.py:472
  2.1 1.7 %collective-permute-start = (f32[48,128]{1,0:T(8,128)S(1)}, f32[48,128]{1,0:T(8,128)S(1)}, u32[]{:S(2)}, u32[]{:S(2)}) collective-permute-start(f32[48,128]{1,0:T(8,128)S(1)} %get-tuple-element.27), channel_id=1, source_target_pairs={{8,16},{16,8},{24,32},{32,24},{40,48},{48,40},{56,64},{64,56},{72,... | collective-permute-start | bytes 73736 | tf_op jit(solution)/shard_map/ppermute | solution.py:452
  3.8 5.4 %collective-permute-start.1 = (f32[48,128]{1,0:T(8,128)S(1)}, f32[48,128]{1,0:T(8,128)S(1)}, u32[]{:S(2)}, u32[]{:S(2)}) collective-permute-start(f32[48,128]{1,0:T(8,128)S(1)} %get-tuple-element.28), channel_id=1, source_target_pairs={{0,8},{8,0},{16,24},{24,16},{32,40},{40,32},{48,56},{56,48},{64,72... | collective-permute-start | bytes 73736 | tf_op jit(solution)/shard_map/ppermute | solution.py:452
  9.1 1.6 %collective-permute-start.2 = (f32[48,128]{1,0:T(8,128)S(1)}, f32[48,128]{1,0:T(8,128)S(1)}, u32[]{:S(2)}, u32[]{:S(2)}) collective-permute-start(f32[48,128]{1,0:T(8,128)S(1)} %get-tuple-element.29), channel_id=1, source_target_pairs={{1,2},{2,1},{3,4},{4,3},{5,6},{6,5},{7,0},{0,7},{9,10},{10,9},{11,... | collective-permute-start | bytes 73736 | tf_op jit(solution)/shard_map/ppermute | solution.py:452
  10.8 0.0 collective-permute-start.3
  10.8 1.7 %shard_map.96 = (f32[96,128]{1,0:T(8,128)S(1)}, f32[48,128]{1,0:T(8,128)S(1)}, f32[96,128]{1,0:T(8,128)S(1)}, bf16[192,256]{1,0:T(8,128)(2,1)S(1)}) custom-call(f32[96,128]{1,0:T(8,128)S(1)} %get-tuple-element.31.fl, f32[48,128]{1,0:T(8,128)S(1)} %get-tuple-element.32.co, f32[48,128]{1,0:T(8,128)S(1)} %get-tuple-element.33.ve, ...), custom_call_target="tpu_custom_call" | custom-call | flops 2147483648 | tf_op jit(solution)/shard_map/pallas_call | solution.py:481
  12.5 0.0 collective-permute-done.r0
  12.5 0.0 collective-permute-done.1.r1
  12.5 1.1 %collective-permute-done.2.r2 = f32[48,128]{1,0:T(8,128)S(1)} collective-permute-done((f32[48,128]{1,0:T(8,128)S(1)}, f32[48,128]{1,0:T(8,128)S(1)}, u32[]{:S(2)}, u32[]{:S(2)}) %collective-permute-start.2) | collective-permute-done | bytes 24608 | tf_op jit(solution)/shard_map/ppermute | solution.py:452
  13.6 0.0 collective-permute-done.3.r3
  13.6 1.8 %shard_map.97 = (f32[96,128]{1,0:T(8,128)S(1)}, f32[96,128]{1,0:T(8,128)S(1)}, f32[32,128]{1,0:T(8,128)S(1)}, f32[32,128]{1,0:T(8,128)S(1)}, f32[32,128]{1,0:T(8,128)S(1)}, /*index=5*/f32[32,128]{1,0:T(8,128)S(1)}) custom-call(f32[48,128]{1,0:T(8,128)S(1)} %collective-permute-done.r0, f32[48,128]{1,0:T(8,128)S(1)} %collective-permute-done.1.r1, ...), custom_call_target="tpu_custom_call" | custom-call | tf_op jit(solution)/shard_map/pallas_call | solution.py:487
  15.4 0.1 collective-permute-start.4
  15.5 2.7 %collective-permute-start.5 = (f32[32,128]{1,0:T(8,128)S(1)}, f32[32,128]{1,0:T(8,128)S(1)}, u32[]{:S(2)}, u32[]{:S(2)}) collective-permute-start(f32[32,128]{1,0:T(8,128)S(1)} %get-tuple-element.44), channel_id=1, source_target_pairs={{0,8},{8,0},{16,24},{24,16},{32,40},{40,32},{48,56},{56,48},{64,72... | collective-permute-start | bytes 49160 | tf_op jit(solution)/shard_map/ppermute | solution.py:452
  18.2 0.5 %collective-permute-start.6 = (f32[32,128]{1,0:T(8,128)S(1)}, f32[32,128]{1,0:T(8,128)S(1)}, u32[]{:S(2)}, u32[]{:S(2)}) collective-permute-start(f32[32,128]{1,0:T(8,128)S(1)} %get-tuple-element.45), channel_id=1, source_target_pairs={{1,2},{2,1},{3,4},{4,3},{5,6},{6,5},{7,0},{0,7},{9,10},{10,9},{11,... | collective-permute-start | bytes 49160 | tf_op jit(solution)/shard_map/ppermute | solution.py:452
  18.7 1.1 %collective-permute-start.7 = (f32[32,128]{1,0:T(8,128)S(1)}, f32[32,128]{1,0:T(8,128)S(1)}, u32[]{:S(2)}, u32[]{:S(2)}) collective-permute-start(f32[32,128]{1,0:T(8,128)S(1)} %get-tuple-element.46), channel_id=1, source_target_pairs={{0,1},{1,0},{2,3},{3,2},{4,5},{5,4},{6,7},{7,6},{8,9},{9,8},{10,11... | collective-permute-start | bytes 49160 | tf_op jit(solution)/shard_map/ppermute | solution.py:452
  19.8 0.2 shard_map.98.base
  20.0 0.0 collective-permute-done.4.r0
  20.0 0.0 collective-permute-done.5.r1
  20.0 2.6 %collective-permute-done.6.r2 = f32[32,128]{1,0:T(8,128)S(1)} collective-permute-done((f32[32,128]{1,0:T(8,128)S(1)}, f32[32,128]{1,0:T(8,128)S(1)}, u32[]{:S(2)}, u32[]{:S(2)}) %collective-permute-start.6) | collective-permute-done | bytes 16416 | tf_op jit(solution)/shard_map/ppermute | solution.py:452
  22.6 0.0 collective-permute-done.7.r3
  22.6 0.9 %shard_map.99 = (f32[96,128]{1,0:T(8,128)}, f32[48,128]{1,0:T(8,128)}) custom-call(f32[32,128]{1,0:T(8,128)S(1)} %collective-permute-done.4.r0, f32[32,128]{1,0:T(8,128)S(1)} %collective-permute-done.5.r1, f32[32,128]{1,0:T(8,128)S(1)} %collective-permute-done.6.r2, f32[32,128]{1,0:T(8,128)S(1)} %collective-permute-done.7.r3, f32[96,128]{1,0:T(8,128)S(1)} %shard_map.98.base, ...), custom_call_target="tpu_custom_call" | custom-call | tf_op jit(solution)/shard_map/pallas_call | solution.py:492
Async XLA Ops:
  2.1 10.4 %collective-permute-start = (f32[48,128]{1,0:T(8,128)S(1)}, f32[48,128]{1,0:T(8,128)S(1)}, u32[]{:S(2)}, u32[]{:S(2)}) collective-permute-start(f32[48,128]{1,0:T(8,128)S(1)} %get-tuple-element.27), channel_id=1, source_target_pairs={{8,16},{16,8},{24,32},{32,24},{40,48},{48,40},{56,64},{64,56},{72,... | collective-permute-start | bytes 73736 | tf_op jit(solution)/shard_map/ppermute | solution.py:452
  3.8 8.7 %collective-permute-start.1 = (f32[48,128]{1,0:T(8,128)S(1)}, f32[48,128]{1,0:T(8,128)S(1)}, u32[]{:S(2)}, u32[]{:S(2)}) collective-permute-start(f32[48,128]{1,0:T(8,128)S(1)} %get-tuple-element.28), channel_id=1, source_target_pairs={{0,8},{8,0},{16,24},{24,16},{32,40},{40,32},{48,56},{56,48},{64,72... | collective-permute-start | bytes 73736 | tf_op jit(solution)/shard_map/ppermute | solution.py:452
  9.1 4.5 %collective-permute-start.2 = (f32[48,128]{1,0:T(8,128)S(1)}, f32[48,128]{1,0:T(8,128)S(1)}, u32[]{:S(2)}, u32[]{:S(2)}) collective-permute-start(f32[48,128]{1,0:T(8,128)S(1)} %get-tuple-element.29), channel_id=1, source_target_pairs={{1,2},{2,1},{3,4},{4,3},{5,6},{6,5},{7,0},{0,7},{9,10},{10,9},{11,... | collective-permute-start | bytes 73736 | tf_op jit(solution)/shard_map/ppermute | solution.py:452
  10.8 2.8 %collective-permute-start.3 = (f32[48,128]{1,0:T(8,128)S(1)}, f32[48,128]{1,0:T(8,128)S(1)}, u32[]{:S(2)}, u32[]{:S(2)}) collective-permute-start(f32[48,128]{1,0:T(8,128)S(1)} %get-tuple-element.30), channel_id=1, source_target_pairs={{0,1},{1,0},{2,3},{3,2},{4,5},{5,4},{6,7},{7,6},{8,9},{9,8},{10,11... | collective-permute-start | bytes 73736 | tf_op jit(solution)/shard_map/ppermute | solution.py:452
  15.4 4.6 %collective-permute-start.4 = (f32[32,128]{1,0:T(8,128)S(1)}, f32[32,128]{1,0:T(8,128)S(1)}, u32[]{:S(2)}, u32[]{:S(2)}) collective-permute-start(f32[32,128]{1,0:T(8,128)S(1)} %get-tuple-element.43), channel_id=1, source_target_pairs={{8,16},{16,8},{24,32},{32,24},{40,48},{48,40},{56,64},{64,56},{72,... | collective-permute-start | bytes 49160 | tf_op jit(solution)/shard_map/ppermute | solution.py:452
  15.5 4.5 %collective-permute-start.5 = (f32[32,128]{1,0:T(8,128)S(1)}, f32[32,128]{1,0:T(8,128)S(1)}, u32[]{:S(2)}, u32[]{:S(2)}) collective-permute-start(f32[32,128]{1,0:T(8,128)S(1)} %get-tuple-element.44), channel_id=1, source_target_pairs={{0,8},{8,0},{16,24},{24,16},{32,40},{40,32},{48,56},{56,48},{64,72... | collective-permute-start | bytes 49160 | tf_op jit(solution)/shard_map/ppermute | solution.py:452
  18.2 4.4 %collective-permute-start.6 = (f32[32,128]{1,0:T(8,128)S(1)}, f32[32,128]{1,0:T(8,128)S(1)}, u32[]{:S(2)}, u32[]{:S(2)}) collective-permute-start(f32[32,128]{1,0:T(8,128)S(1)} %get-tuple-element.45), channel_id=1, source_target_pairs={{1,2},{2,1},{3,4},{4,3},{5,6},{6,5},{7,0},{0,7},{9,10},{10,9},{11,... | collective-permute-start | bytes 49160 | tf_op jit(solution)/shard_map/ppermute | solution.py:452
  18.7 3.9 %collective-permute-start.7 = (f32[32,128]{1,0:T(8,128)S(1)}, f32[32,128]{1,0:T(8,128)S(1)}, u32[]{:S(2)}, u32[]{:S(2)}) collective-permute-start(f32[32,128]{1,0:T(8,128)S(1)} %get-tuple-element.46), channel_id=1, source_target_pairs={{0,1},{1,0},{2,3},{3,2},{4,5},{5,4},{6,7},{7,6},{8,9},{9,8},{10,11... | collective-permute-start | bytes 49160 | tf_op jit(solution)/shard_map/ppermute | solution.py:452

commit v3 on v2

--- a/solution.py
+++ b/solution.py
@@ -142,25 +142,24 @@
     return x_lo, x_hi, jnp.concatenate(y_lo, axis=0), jnp.concatenate(y_hi, axis=0)
 
 
-def received_faces(odd_d, odd_c, drift_odd, drift_even, cross_odd, cross_even):
+def face_part(along, up, message):
     m = face_masks()
-    from_hi_x = jnp.where(odd_d, drift_odd, drift_even)
-    from_lo_x = jnp.where(odd_d, drift_even, drift_odd)
-    from_hi_y = jnp.where(odd_c, cross_odd, cross_even)
-    from_lo_y = jnp.where(odd_c, cross_even, cross_odd)
-    hi_y = [pltpu.roll(from_hi_y[8 * g : 8 * g + 8], 56, 1) for g in range(2)]
-    lo_y = [from_lo_y[8 * g : 8 * g + 8] for g in range(2)]
+    if along == "drift":
+        sides = (jnp.where(up, 0.0, m["x_lo"]), jnp.where(up, m["x_hi"], 0.0))
+
+        def at(c, x, z):
+            r = 2 * (c * 2 + z)
+            return jnp.concatenate([message[r : r + 2]] * 4, axis=0) * sides[x]
+
+        return at
+    side = jnp.where(up, m["y_hi"], m["y_lo"])
+    pieces = [message[8 * g : 8 * g + 8] for g in range(2)]
+    pieces = [jnp.where(up, pltpu.roll(v, 56, 1), v) for v in pieces]
 
     def at(c, x, z):
-        r = 2 * (c * 2 + z)
-        rows = (from_hi_x if x == 1 else from_lo_x)[r : r + 2]
-        out = jnp.concatenate([rows] * 4, axis=0) * (m["x_hi"] if x == 1 else m["x_lo"])
         index = (c * 2 + x) * 2 + z
         g, i = index // 6, index % 6
-        back = (128 - 8 * i) % 128
-        hi = pltpu.roll(hi_y[g], back, 1) if back else hi_y[g]
-        lo = pltpu.roll(lo_y[g], back, 1) if back else lo_y[g]
-        return out + hi * m["y_hi"] + lo * m["y_lo"]
+        return (pltpu.roll(pieces[g], 128 - 8 * i, 1) if i else pieces[g]) * side
 
     return at
 
@@ -211,7 +210,7 @@
     return jnp.concatenate([rows, rows], axis=1)
 
 
-def couple(n_tiles, coords_at, velocity_at, drag_at, host_at, field, emit, base, wts, ra, group=4):
+def couple(n_tiles, coords_at, velocity_at, drag_at, host_at, field, emit, base, wts, ra, group=8):
     even = node_tables([0, 0, 2, 2, 4, 4, 6, 6])
     odd = node_tables([1, 1, 3, 3, 5, 5, 7, 7])
     plain = node_tables(list(range(8)))
@@ -274,25 +273,54 @@
     return jnp.where(iota((96, 128), 1) < 64, d[0:96], d[96:192])
 
 
-def lists_onehot(mig, store):
+ALONG = ("drift", "drift", "cross", "cross")
+FACES = 32
+BACK = 16
+
+
+def ups():
+    odd_d, odd_c = parity("drift"), parity("cross")
+    return odd_d, jnp.logical_not(odd_d), odd_c, jnp.logical_not(odd_c)
+
+
+def towards(s, up):
+    return 2 * (s // 2) + up.astype(jnp.int32)
+
+
+def faces_to(s, up, packed):
+    low, high = packed[2 * (s // 2) : 2 * (s // 2) + 2]
+    return jnp.where(up, high, low)
+
+
+def gather(s, hi_lo, lists, onehot, out):
+    lane_row = iota((128, 128), 0)
     high = []
-    lane_row = iota((128, 128), 0)
-    for t in range(16):
-        idx = mig[t : t + 1, :]
-        store[:, 128 * t : 128 * t + 128] = jnp.where(lane_row == (idx & 127), 1.0, 0.0).astype(BF16)
+    for t in range(4):
+        idx = lists[4 * s + t : 4 * s + t + 1, :]
+        cols = slice(512 * s + 128 * t, 512 * s + 128 * t + 128)
+        onehot[:, cols] = jnp.where(lane_row == (idx & 127), 1.0, 0.0).astype(BF16)
         high.append(idx >> 7)
-    return high
+    span = onehot[:, 512 * s : 512 * s + 512]
+    y = jnp.dot(hi_lo, jnp.concatenate([span, span], axis=0), preferred_element_type=F32)
+    for t in range(4):
+        g = jnp.zeros((8, 128), F32)
+        for row in range(16):
+            g = jnp.where(high[t] == row, y[8 * row : 8 * row + 8, 128 * t : 128 * t + 128], g)
+        out[8 * t : 8 * t + 8, :] = g
 
 
 def send_kernel(
-    fl, co, ve, dr, ho, mi, ta, la, o0, o1, o2, o3, vf, vc, vv, vd, vh, vm, vt, vl, onehot, table, sems
+    fl, co, ve, dr, ho, mi, ta, la, o0, o1, o2, o3, vf, vc, vv, vd, vh, lists, vt, vl, onehot, vm, table, sems
 ):
     pairs = ((mi, vm), (co, vc), (ve, vv), (dr, vd), (ho, vh), (fl, vf), (ta, vt), (la, vl))
     copies = [pltpu.make_async_copy(src, dst, sems.at[n]) for n, (src, dst) in enumerate(pairs)]
     for copy in copies:
         copy.start()
+    up = ups()
     copies[0].wait()
-    high = lists_onehot(vm, onehot)
+    for s in range(4):
+        for t in range(4):
+            lists[4 * s + t : 4 * s + t + 1, :] = vm[pl.ds(4 * t + towards(s, up[s]), 1), :]
     for copy in copies[1:]:
         copy.wait()
     for c in range(3):
@@ -300,37 +328,19 @@
         table[pl.ds(3 + c, 16, stride=8), :] = vv[16 * c : 16 * c + 16, :]
     table[pl.ds(6, 16, stride=8), :] = vd[...]
     table[pl.ds(7, 16, stride=8), :] = vh[...].astype(F32)
-    hi, lo = split(table[...])
-    hi_lo = jnp.concatenate([hi, lo], axis=1)
-    odd_d, odd_c = parity("drift"), parity("cross")
-    x_lo, x_hi, y_lo, y_hi = pack_faces(functools.partial(tile_of, vf))
-    o0[32:48, :] = jnp.where(odd_d, x_hi, x_lo)
-    o1[32:48, :] = jnp.where(odd_d, x_lo, x_hi)
-    o2[32:48, :] = jnp.where(odd_c, y_hi, y_lo)
-    o3[32:48, :] = jnp.where(odd_c, y_lo, y_hi)
-    for t in range(4):
-        span = onehot[:, 512 * t : 512 * t + 512]
-        y = jnp.dot(hi_lo, jnp.concatenate([span, span], axis=0), preferred_element_type=F32)
-        found = []
-        for d in range(4):
-            h = high[4 * t + d]
-            g = jnp.zeros((8, 128), F32)
-            for row in range(16):
-                g = jnp.where(h == row, y[8 * row : 8 * row + 8, 128 * d : 128 * d + 128], g)
-            found.append(g)
-        rows = slice(8 * t, 8 * t + 8)
-        o0[rows, :] = jnp.where(odd_d, found[1], found[0])
-        o1[rows, :] = jnp.where(odd_d, found[0], found[1])
-        o2[rows, :] = jnp.where(odd_c, found[3], found[2])
-        o3[rows, :] = jnp.where(odd_c, found[2], found[3])
+    parts = jnp.concatenate(split(table[...]), axis=1)
+    packed = pack_faces(functools.partial(tile_of, vf))
+    for s, out in enumerate((o0, o1, o2, o3)):
+        out[FACES:, :] = faces_to(s, up[s], packed)
+        gather(s, parts, lists, onehot, out)
 
 
 def own_kernel(
-    fl, co, ve, dr, ho, mi, tab, lane_op, onehot, dep_out, vel_out, base_out, operand_out, car, base, wts, ra
+    fl, co, ve, dr, ho, lists, tab, lane_op, onehot, dep_out, vel_out, base_out, operand_out, car, base, wts, ra
 ):
-    high = [mi[t : t + 1, :] >> 7 for t in range(16)]
     sub16 = iota((16, 128), 0)
-    rows = jnp.concatenate([jnp.where(h == sub16, 1.0, 0.0) for h in high], axis=1).astype(BF16)
+    rows = [jnp.where((lists[t : t + 1, :] >> 7) == sub16, 1.0, 0.0) for t in range(16)]
+    rows = jnp.concatenate(rows, axis=1).astype(BF16)
     listed = lax.dot_general(rows, onehot[...], (((1,), (1,)), ((), ())), preferred_element_type=F32)
     own = jnp.where(listed > 0.5, 0.0, 1.0)
     get = functools.partial(tile_of, fl)
@@ -358,36 +368,43 @@
         base_out[8 * n : 8 * n + 8, :] = out[i]
 
 
-def host_kernel(r0, r1, r2, r3, operand, dep_in, base_in, u_out, dep_out, o0, o1, o2, o3, base, wts, ra):
-    received, sent = (r0, r1, r2, r3), (o0, o1, o2, o3)
-    odd_d, odd_c = parity("drift"), parity("cross")
+def host_lists(received, back, dep_in, operand, scratch):
     pick = lambda t, v: row_of(received[t // 4], 8 * (t % 4) + v)
 
     def emit(t, carried):
-        for c in range(3):
-            sent[t // 4][4 * (t % 4) + c : 4 * (t % 4) + c + 1, :] = carried[c]
-        sent[t // 4][4 * (t % 4) + 3 : 4 * (t % 4) + 4, :] = carried[0]
-
-    dep = dep_in[...] + couple(
-        16,
+        rows = carried + [carried[0]]
+        for c in range(4):
+            back[t // 4][4 * (t % 4) + c : 4 * (t % 4) + c + 1, :] = rows[c]
+
+    return dep_in[...] + couple(
+        4 * len(received),
         lambda t: [pick(t, c) for c in range(3)],
         lambda t: [pick(t, 3 + c) for c in range(3)],
         lambda t: pick(t, 6),
         lambda t: pick(t, 7).astype(jnp.int32),
-        operand[...], emit, base, wts, ra,
-    )
+        operand[...], emit, *scratch,
+    )
+
+
+def near_kernel(r1, r3, operand, dep_in, dep_out, b1, b3, *scratch):
+    dep_out[...] = host_lists((r1, r3), (b1, b3), dep_in, operand, scratch)
+
+
+def far_kernel(r0, r1, r2, r3, operand, dep_in, base_in, b1, b3, u_out, dep_out, o0, o1, o2, o3, *scratch):
+    dep = host_lists((r0, r2), (o0, o2), dep_in, operand, scratch)
     dep_out[...] = dep
-    faces = received_faces(odd_d, odd_c, *[r[32:48, :] for r in received])
+    up = ups()
+    parts = [face_part(ALONG[s], up[s], r[FACES:, :]) for s, r in enumerate((r0, r1, r2, r3))]
     new = {}
     for n, i in enumerate(CXZ):
         r = slice(8 * n, 8 * n + 8)
-        new[i] = base_in[r, :] + faces(*i) + 0.5 * dep[r]
+        new[i] = base_in[r, :] + sum(part(*i) for part in parts) + 0.5 * dep[r]
         u_out[r, :] = new[i]
-    x_lo, x_hi, y_lo, y_hi = pack_faces(lambda c, x, z: new[c, x, z])
-    o0[16:32, :] = jnp.where(odd_d, x_hi, x_lo)
-    o1[16:32, :] = jnp.where(odd_d, x_lo, x_hi)
-    o2[16:32, :] = jnp.where(odd_c, y_hi, y_lo)
-    o3[16:32, :] = jnp.where(odd_c, y_lo, y_hi)
+    packed = pack_faces(lambda c, x, z: new[c, x, z])
+    o1[0:BACK, :] = b1[...]
+    o3[0:BACK, :] = b3[...]
+    for s, out in enumerate((o0, o1, o2, o3)):
+        out[BACK:, :] = faces_to(s, up[s], packed)
 
 
 def second_kernel(u, dep, tab, lane_op, out_ref):
@@ -397,29 +414,21 @@
         out_ref[r, :] = out[i] + 0.5 * dep[r, :]
 
 
-def last_kernel(r0, r1, r2, r3, base, vel, dr, mi, onehot, fluid_out, vel_out):
-    odd_d, odd_c = parity("drift"), parity("cross")
-    faces = received_faces(odd_d, odd_c, *[r[16:32, :] for r in (r0, r1, r2, r3)])
+def last_kernel(r0, r1, r2, r3, base, vel, dr, lists, onehot, fluid_out, vel_out):
+    received = [r[...] for r in (r0, r1, r2, r3)]
+    up = ups()
+    parts = [face_part(ALONG[s], up[s], received[s][BACK:]) for s in range(4)]
     for n, i in enumerate(CXZ):
-        r = slice(8 * n, 8 * n + 8)
-        fluid_out[r, :] = base[r, :] + faces(*i)
+        fluid_out[8 * n : 8 * n + 8, :] = tile_of(base, *i) + sum(part(*i) for part in parts)
     sub16 = iota((16, 128), 0)
     columns = []
-    for t in range(4):
-        rows = slice(4 * t, 4 * t + 4)
-        back = [
-            jnp.where(odd_d, r1[rows, :], r0[rows, :]),
-            jnp.where(odd_d, r0[rows, :], r1[rows, :]),
-            jnp.where(odd_c, r3[rows, :], r2[rows, :]),
-            jnp.where(odd_c, r2[rows, :], r3[rows, :]),
-        ]
-        for d in range(4):
-            at = (mi[4 * t + d : 4 * t + d + 1, :] >> 7) == sub16
-            columns.append(jnp.concatenate([jnp.where(at, back[d][c : c + 1], 0.0) for c in range(3)], axis=0))
-    hi, lo = split(jnp.concatenate(columns, axis=1))
-    put = lax.dot_general(
-        jnp.concatenate([hi, lo], axis=0), onehot[...], (((1,), (1,)), ((), ())), preferred_element_type=F32
-    )
+    for s in range(4):
+        for t in range(4):
+            at = (lists[4 * s + t : 4 * s + t + 1, :] >> 7) == sub16
+            back = received[s][4 * t : 4 * t + 4]
+            columns.append(jnp.concatenate([jnp.where(at, back[c : c + 1], 0.0) for c in range(3)], axis=0))
+    rows = jnp.concatenate(split(jnp.concatenate(columns, axis=1)), axis=0)
+    put = lax.dot_general(rows, onehot[...], (((1,), (1,)), ((), ())), preferred_element_type=F32)
     put = put[0:48] + put[48:96]
     for c in range(3):
         r = slice(16 * c, 16 * c + 16)
@@ -443,18 +452,23 @@
     )
 
 
-def swap(block, axis, odd):
-    count = lax.axis_size(axis)
-    pairs = []
-    for i in range(odd, count + odd, 2):
-        first, other = i % count, (i + 1) % count
-        pairs += [(first, other), (other, first)]
-    return lax.ppermute(block, axis, pairs)
-
-
-def exchange(blocks):
-    order = (("drift", 1), ("drift", 0), ("cross", 1), ("cross", 0))
-    return [swap(block, axis, odd) for block, (axis, odd) in zip(blocks, order)]
+def exchange(messages):
+    rows, columns = lax.axis_size("drift"), lax.axis_size("cross")
+
+    def partner(i, j, s):
+        if s < 2:
+            return (i + (1 if i % 2 != s else -1)) % rows, j
+        return i, (j + (1 if j % 2 != s - 2 else -1)) % columns
+
+    received = []
+    for n, message in enumerate(messages):
+        pairs = []
+        for i in range(rows):
+            for j in range(columns):
+                k, l = partner(i, j, n)
+                pairs.append((i * columns + j, k * columns + l))
+        received.append(lax.ppermute(message, ("drift", "cross"), pairs))
+    return received
 
 
 def per_device(fluid_field, coords, velocity, drag_factor, host_ids, migrants):
@@ -467,29 +481,41 @@
         host_ids.reshape(16, 128),
         migrants.reshape(4, 4, 128).transpose(1, 0, 2).reshape(16, 128),
     )
-    couple_scratch = [pltpu.VMEM((16, 2048), F32), pltpu.VMEM((256, 2048), BF16), pltpu.VMEM((384, 2048), BF16)]
     args += tuple(jnp.asarray(t) for t in operator_tables())
+    back = shape(BACK)
+
+    def scratch(tiles):
+        n = 128 * tiles
+        return [pltpu.VMEM((16, n), F32), pltpu.VMEM((256, n), BF16), pltpu.VMEM((384, n), BF16)]
+
     outs = call(
         send_kernel,
-        [shape(48)] * 4 + [shape(*a.shape[:1], a.dtype, a.shape[1]) for a in args] + [shape(128, BF16, 2048)],
-        [pltpu.VMEM((128, 128), F32), pltpu.SemaphoreType.DMA((8,))],
+        [shape(48)] * 4
+        + [shape(a.shape[0], a.dtype, a.shape[1]) for a in args]
+        + [shape(128, BF16, 2048)],
+        [
+            pltpu.VMEM((16, 128), jnp.int32),
+            pltpu.VMEM((128, 128), F32),
+            pltpu.SemaphoreType.DMA((8,)),
+        ],
         in_specs=[pl.BlockSpec(memory_space=pl.ANY)] * 8,
     )(*(pltpu.with_memory_space_constraint(a, pltpu.HBM) for a in args))
     sends, args, onehot = outs[:4], outs[4:12], outs[12]
-    tab, lane_op = args[6:]
-    received = exchange(sends)
+    drag, lists, tab, lane_op = args[3], *args[5:]
+    r0, r1, r2, r3 = exchange(sends)
     dep, vel, base, operand = call(
         own_kernel,
         [shape(96), shape(48), shape(96), shape(192, BF16, 256)],
-        [pltpu.VMEM((48, 128), F32)] + couple_scratch,
+        [pltpu.VMEM((48, 128), F32)] + scratch(16),
         cost=1 << 31,
     )(*args, onehot)
-    u, dep, *sends = call(host_kernel, [shape(96)] * 2 + [shape(32)] * 4, couple_scratch)(
-        *received, operand, dep, base
+    dep, *rest = call(near_kernel, [shape(96)] + [back] * 2, scratch(8), cost=1 << 30)(r1, r3, operand, dep)
+    u, dep, *sends = call(far_kernel, [shape(96)] * 2 + [shape(32)] * 4, scratch(8))(
+        r0, r1, r2, r3, operand, dep, base, *rest
     )
     received = exchange(sends)
     base = call(second_kernel, shape(96), cost=1 << 30)(u, dep, tab, lane_op)
-    fluid, vel = call(last_kernel, [shape(96), shape(48)])(*received, base, vel, args[3], args[5], onehot)
+    fluid, vel = call(last_kernel, [shape(96), shape(48)])(*received, base, vel, drag, lists, onehot)
     fluid = fluid.reshape(3, 2, 8, 2, 128).transpose(0, 1, 3, 2, 4).reshape(3, 2, 2, 1024)
     return fluid, vel.reshape(3, 1, 1, 2048)
 

time: 23.6 us -> 22.8 us (0.966)
  the two profiles are of different devices: /device:TPU:8 before, /device:TPU:1 now
where the time goes in v3:
time: 22.8 us; the launch traced here: 22.6 us
  starting transfers between devices  13.9 us (61%)
  Pallas kernels  6.1 us (27%)
  waiting for transfers between devices  1.96 us (9%)
  between operations  0.71 us (3%)
    ppermute x8, starting transfers between devices, exchange(): received.append(lax.ppermute(message, ('drift', 'cross'), pairs))  13.9 us
    ppermute x8, waiting for transfers between devices, exchange(): received.append(lax.ppermute(message, ('drift', 'cross'), pairs))  1.96 us
    pallas_call x1, Pallas kernels, per_device(): call(own_kernel, [shape(96), shape(48), shape(96), shape(192, BF16, 256)]...  1.59 us
    pallas_call x1, Pallas kernels, per_device(): call(send_kernel, [shape(48)] * 4 + [shape(a.shape[0], a.dtype, a.shape[1...  1.53 us
    pallas_call x1, Pallas kernels, per_device(): call(far_kernel, [shape(96)] * 2 + [shape(32)] * 4, scratch(8))  0.98 us
    pallas_call x1, Pallas kernels, per_device(): call(last_kernel, [shape(96), shape(48)])  0.93 us
    pallas_call x1, Pallas kernels, per_device(): call(near_kernel, [shape(96)] + [back] * 2, scratch(8), cost=1 << 30)  0.9 us
  transfers between devices with their start and end apart: 8, of which 1 were waited for; matrix products, arithmetic and copies ran while one was open for 0% of the time, Pallas kernels for 12%

profile of v3, /device:TPU:1, one launch (start us, length us, event | category | flops | bytes accessed | tf_op | source)
XLA Modules:
  0.0 22.6 jit_solution(3179903103789588752)
XLA Ops:
  0.6 1.5 %shard_map.95 = (f32[48,128]{1,0:T(8,128)S(1)}, f32[48,128]{1,0:T(8,128)S(1)}, f32[48,128]{1,0:T(8,128)S(1)}, f32[48,128]{1,0:T(8,128)S(1)}, f32[96,128]{1,0:T(8...) custom-call(f32[96,128]{1,0:T(8,128)} %bitcast.20, ...), custom_call_target="tpu_custom_call" | custom-call | tf_op jit(solution)/shard_map/pallas_call | solution.py:491
  2.2 7.1 %collective-permute-start = (f32[48,128]{1,0:T(8,128)S(1)}, f32[48,128]{1,0:T(8,128)S(1)}, u32[]{:S(2)}, u32[]{:S(2)}) collective-permute-start(f32[48,128]{1,0:T(8,128)S(1)} %get-tuple-element.30), channel_id=1, source_target_pairs={{0,120},{1,121},{2,122},{3,123},{4,124},{5,125},{6,126},{7,127},{8... | collective-permute-start | bytes 73736 | tf_op jit(solution)/shard_map/ppermute | solution.py:470
  9.3 0.0 collective-permute-start.1
  9.3 2.1 %collective-permute-start.2 = (f32[48,128]{1,0:T(8,128)S(1)}, f32[48,128]{1,0:T(8,128)S(1)}, u32[]{:S(2)}, u32[]{:S(2)}) collective-permute-start(f32[48,128]{1,0:T(8,128)S(1)} %get-tuple-element.32), channel_id=1, source_target_pairs={{0,7},{1,2},{2,1},{3,4},{4,3},{5,6},{6,5},{7,0},{8,15},{9,10},{10,... | collective-permute-start | bytes 73736 | tf_op jit(solution)/shard_map/ppermute | solution.py:470
  11.3 0.8 %collective-permute-start.3 = (f32[48,128]{1,0:T(8,128)S(1)}, f32[48,128]{1,0:T(8,128)S(1)}, u32[]{:S(2)}, u32[]{:S(2)}) collective-permute-start(f32[48,128]{1,0:T(8,128)S(1)} %get-tuple-element.33), channel_id=1, source_target_pairs={{0,1},{1,0},{2,3},{3,2},{4,5},{5,4},{6,7},{7,6},{8,9},{9,8},{10,11... | collective-permute-start | bytes 73736 | tf_op jit(solution)/shard_map/ppermute | solution.py:470
  12.2 1.6 %shard_map.96 = (f32[96,128]{1,0:T(8,128)S(1)}, f32[48,128]{1,0:T(8,128)S(1)}, f32[96,128]{1,0:T(8,128)S(1)}, bf16[192,256]{1,0:T(8,128)(2,1)S(1)}) custom-call(f32[96,128]{1,0:T(8,128)S(1)} %get-tuple-element.34.fl, f32[48,128]{1,0:T(8,128)S(1)} %get-tuple-element.35.co, f32[48,128]{1,0:T(8,128)S(1)} %get-tuple-element.36.ve, ...), custom_call_target="tpu_custom_call" | custom-call | flops 2147483648 | tf_op jit(solution)/shard_map/pallas_call | solution.py:506
  13.8 0.0 collective-permute-done.1.r1
  13.8 0.0 collective-permute-done.3.r3
  13.8 0.9 %shard_map.97 = (f32[96,128]{1,0:T(8,128)S(1)}, f32[16,128]{1,0:T(8,128)S(1)}, f32[16,128]{1,0:T(8,128)S(1)}) custom-call(f32[48,128]{1,0:T(8,128)S(1)} %collective-permute-done.1.r1, f32[48,128]{1,0:T(8,128)S(1)} %collective-permute-done.3.r3, bf16[192,256]{1,0:T(8,128)(2,1)S(1)} %get-tuple-element.43.operand, f32[96,128]{1,0:T(8,128)S(1)} %get-tuple-element.44.dep_in), custom_call_target="tpu_custom_call" | custom-call | flops 1073741824 | tf_op jit(solution)/shard_map/pallas_call | solution.py:512
  14.7 0.0 collective-permute-done.r0
  14.7 0.0 collective-permute-done.2.r2
  14.7 1.0 %shard_map.98 = (f32[96,128]{1,0:T(8,128)S(1)}, f32[96,128]{1,0:T(8,128)S(1)}, f32[32,128]{1,0:T(8,128)S(1)}, f32[32,128]{1,0:T(8,128)S(1)}, f32[32,128]{1,0:T(8,128)S(1)}, /*index=5*/f32[32,128]{1,0:T(8,128)S(1)}) custom-call(f32[48,128]{1,0:T(8,128)S(1)} %collective-permute-done.r0, f32[48,128]{1,0:T(8,128)S(1)} %collective-permute-done.1.r1, ...), custom_call_target="tpu_custom_call" | custom-call | tf_op jit(solution)/shard_map/pallas_call | solution.py:513
  15.7 0.7 %collective-permute-start.4 = (f32[32,128]{1,0:T(8,128)S(1)}, f32[32,128]{1,0:T(8,128)S(1)}, u32[]{:S(2)}, u32[]{:S(2)}) collective-permute-start(f32[32,128]{1,0:T(8,128)S(1)} %get-tuple-element.49), channel_id=1, source_target_pairs={{0,120},{1,121},{2,122},{3,123},{4,124},{5,125},{6,126},{7,127},{8... | collective-permute-start | bytes 49160 | tf_op jit(solution)/shard_map/ppermute | solution.py:470
  16.4 0.9 %collective-permute-start.5 = (f32[32,128]{1,0:T(8,128)S(1)}, f32[32,128]{1,0:T(8,128)S(1)}, u32[]{:S(2)}, u32[]{:S(2)}) collective-permute-start(f32[32,128]{1,0:T(8,128)S(1)} %get-tuple-element.50), channel_id=1, source_target_pairs={{0,8},{1,9},{2,10},{3,11},{4,12},{5,13},{6,14},{7,15},{8,0},{9,1},... | collective-permute-start | bytes 49160 | tf_op jit(solution)/shard_map/ppermute | solution.py:470
  17.3 2.2 %collective-permute-start.6 = (f32[32,128]{1,0:T(8,128)S(1)}, f32[32,128]{1,0:T(8,128)S(1)}, u32[]{:S(2)}, u32[]{:S(2)}) collective-permute-start(f32[32,128]{1,0:T(8,128)S(1)} %get-tuple-element.51), channel_id=1, source_target_pairs={{0,7},{1,2},{2,1},{3,4},{4,3},{5,6},{6,5},{7,0},{8,15},{9,10},{10,... | collective-permute-start | bytes 49160 | tf_op jit(solution)/shard_map/ppermute | solution.py:470
  19.6 0.0 collective-permute-start.7
  19.6 0.2 shard_map.99.base
  19.7 1.9 %collective-permute-done.4.r0 = f32[32,128]{1,0:T(8,128)S(1)} collective-permute-done((f32[32,128]{1,0:T(8,128)S(1)}, f32[32,128]{1,0:T(8,128)S(1)}, u32[]{:S(2)}, u32[]{:S(2)}) %collective-permute-start.4) | collective-permute-done | bytes 16416 | tf_op jit(solution)/shard_map/ppermute | solution.py:470
  21.7 0.0 collective-permute-done.5.r1
  21.7 0.0 collective-permute-done.6.r2
  21.7 0.0 collective-permute-done.7.r3
  21.7 0.9 %shard_map.100 = (f32[96,128]{1,0:T(8,128)}, f32[48,128]{1,0:T(8,128)}) custom-call(f32[32,128]{1,0:T(8,128)S(1)} %collective-permute-done.4.r0, f32[32,128]{1,0:T(8,128)S(1)} %collective-permute-done.5.r1, f32[32,128]{1,0:T(8,128)S(1)} %collective-permute-done.6.r2, f32[32,128]{1,0:T(8,128)S(1)} %collective-permute-done.7.r3, ...), custom_call_target="tpu_custom_call" | custom-call | tf_op jit(solution)/shard_map/pallas_call | solution.py:518
Async XLA Ops:
  2.2 12.5 %collective-permute-start = (f32[48,128]{1,0:T(8,128)S(1)}, f32[48,128]{1,0:T(8,128)S(1)}, u32[]{:S(2)}, u32[]{:S(2)}) collective-permute-start(f32[48,128]{1,0:T(8,128)S(1)} %get-tuple-element.30), channel_id=1, source_target_pairs={{0,120},{1,121},{2,122},{3,123},{4,124},{5,125},{6,126},{7,127},{8... | collective-permute-start | bytes 73736 | tf_op jit(solution)/shard_map/ppermute | solution.py:470
  9.3 4.5 %collective-permute-start.1 = (f32[48,128]{1,0:T(8,128)S(1)}, f32[48,128]{1,0:T(8,128)S(1)}, u32[]{:S(2)}, u32[]{:S(2)}) collective-permute-start(f32[48,128]{1,0:T(8,128)S(1)} %get-tuple-element.31), channel_id=1, source_target_pairs={{0,8},{1,9},{2,10},{3,11},{4,12},{5,13},{6,14},{7,15},{8,0},{9,1},... | collective-permute-start | bytes 73736 | tf_op jit(solution)/shard_map/ppermute | solution.py:470
  9.3 5.4 %collective-permute-start.2 = (f32[48,128]{1,0:T(8,128)S(1)}, f32[48,128]{1,0:T(8,128)S(1)}, u32[]{:S(2)}, u32[]{:S(2)}) collective-permute-start(f32[48,128]{1,0:T(8,128)S(1)} %get-tuple-element.32), channel_id=1, source_target_pairs={{0,7},{1,2},{2,1},{3,4},{4,3},{5,6},{6,5},{7,0},{8,15},{9,10},{10,... | collective-permute-start | bytes 73736 | tf_op jit(solution)/shard_map/ppermute | solution.py:470
  11.3 2.4 %collective-permute-start.3 = (f32[48,128]{1,0:T(8,128)S(1)}, f32[48,128]{1,0:T(8,128)S(1)}, u32[]{:S(2)}, u32[]{:S(2)}) collective-permute-start(f32[48,128]{1,0:T(8,128)S(1)} %get-tuple-element.33), channel_id=1, source_target_pairs={{0,1},{1,0},{2,3},{3,2},{4,5},{5,4},{6,7},{7,6},{8,9},{9,8},{10,11... | collective-permute-start | bytes 73736 | tf_op jit(solution)/shard_map/ppermute | solution.py:470
  15.7 6.0 %collective-permute-start.4 = (f32[32,128]{1,0:T(8,128)S(1)}, f32[32,128]{1,0:T(8,128)S(1)}, u32[]{:S(2)}, u32[]{:S(2)}) collective-permute-start(f32[32,128]{1,0:T(8,128)S(1)} %get-tuple-element.49), channel_id=1, source_target_pairs={{0,120},{1,121},{2,122},{3,123},{4,124},{5,125},{6,126},{7,127},{8... | collective-permute-start | bytes 49160 | tf_op jit(solution)/shard_map/ppermute | solution.py:470
  16.4 5.3 %collective-permute-start.5 = (f32[32,128]{1,0:T(8,128)S(1)}, f32[32,128]{1,0:T(8,128)S(1)}, u32[]{:S(2)}, u32[]{:S(2)}) collective-permute-start(f32[32,128]{1,0:T(8,128)S(1)} %get-tuple-element.50), channel_id=1, source_target_pairs={{0,8},{1,9},{2,10},{3,11},{4,12},{5,13},{6,14},{7,15},{8,0},{9,1},... | collective-permute-start | bytes 49160 | tf_op jit(solution)/shard_map/ppermute | solution.py:470
  17.3 4.4 %collective-permute-start.6 = (f32[32,128]{1,0:T(8,128)S(1)}, f32[32,128]{1,0:T(8,128)S(1)}, u32[]{:S(2)}, u32[]{:S(2)}) collective-permute-start(f32[32,128]{1,0:T(8,128)S(1)} %get-tuple-element.51), channel_id=1, source_target_pairs={{0,7},{1,2},{2,1},{3,4},{4,3},{5,6},{6,5},{7,0},{8,15},{9,10},{10,... | collective-permute-start | bytes 49160 | tf_op jit(solution)/shard_map/ppermute | solution.py:470
  19.6 2.1 %collective-permute-start.7 = (f32[32,128]{1,0:T(8,128)S(1)}, f32[32,128]{1,0:T(8,128)S(1)}, u32[]{:S(2)}, u32[]{:S(2)}) collective-permute-start(f32[32,128]{1,0:T(8,128)S(1)} %get-tuple-element.52), channel_id=1, source_target_pairs={{0,1},{1,0},{2,3},{3,2},{4,5},{5,4},{6,7},{7,6},{8,9},{9,8},{10,11... | collective-permute-start | bytes 49160 | tf_op jit(solution)/shard_map/ppermute | solution.py:470

commit v4 on v3

--- a/solution.py
+++ b/solution.py
@@ -228,11 +228,10 @@
             w = jnp.concatenate([jnp.broadcast_to(lb[b : b + 1], (8, 128)) * lc for b in range(8)], axis=0)
             hi, lo = split(w)
             wts[0:64, cols] = hi
-            wts[64:128, cols] = hi
-            wts[128:192, cols] = lo
-            wts[192:256, cols] = lo
+            wts[64:128, cols] = lo
         span = slice(128 * g * group, 128 * (g + 1) * group)
-        h = jnp.dot(field, wts[:, span], preferred_element_type=F32)
+        hi, lo = wts[0:64, span], wts[64:128, span]
+        h = jnp.dot(field, jnp.concatenate([hi, hi, lo, lo], axis=0), preferred_element_type=F32)
         for t in range(g * group, g * group + group):
             cols = slice(128 * t, 128 * t + 128)
             sub = slice(128 * (t - g * group), 128 * (t - g * group) + 128)
@@ -240,6 +239,8 @@
             q = (code // 4) * 2 + code % 2
             drag = drag_at(t) * (-MASS)
             at = [q == i for i in range(4)]
+            ones = [jnp.where(at[i], 1.0, 0.0) for i in range(4)]
+            ones = [jnp.concatenate(ones[2 * x : 2 * x + 2], axis=0).astype(BF16) for x in range(2)]
             lines = [base[0:8, cols], base[8:16, cols]]
             carried = []
             for c in range(3):
@@ -262,10 +263,11 @@
                     lo = v - hi
                     for part, value in enumerate((hi, lo)):
                         first = ((part * 2 + a1) * 3 + c) * 32
-                        rows = jnp.concatenate([jnp.where(at[i], value, 0.0) for i in range(4)], axis=0)
-                        ra[first : first + 32, cols] = rows.astype(BF16)
+                        twice = jnp.concatenate([value, value], axis=0).astype(BF16)
+                        ra[first : first + 16, cols] = twice * ones[0]
+                        ra[first + 16 : first + 32, cols] = twice * ones[1]
         d = lax.dot_general(
-            ra[:, span], wts[64:192, span], (((1,), (1,)), ((), ())), preferred_element_type=F32
+            ra[:, span], wts[:, span], (((1,), (1,)), ((), ())), preferred_element_type=F32
         )
         total = d if total is None else total + d
     d = total[0:192] + total[192:384]
@@ -292,20 +294,21 @@
     return jnp.where(up, high, low)
 
 
+def mark(lists, onehot):
+    lane_row = iota((128, 128), 0)
+    for t in range(16):
+        low = lists[t : t + 1, :] & 127
+        onehot[:, 128 * t : 128 * t + 128] = jnp.where(lane_row == low, 1.0, 0.0).astype(BF16)
+
+
 def gather(s, hi_lo, lists, onehot, out):
-    lane_row = iota((128, 128), 0)
-    high = []
-    for t in range(4):
-        idx = lists[4 * s + t : 4 * s + t + 1, :]
-        cols = slice(512 * s + 128 * t, 512 * s + 128 * t + 128)
-        onehot[:, cols] = jnp.where(lane_row == (idx & 127), 1.0, 0.0).astype(BF16)
-        high.append(idx >> 7)
     span = onehot[:, 512 * s : 512 * s + 512]
     y = jnp.dot(hi_lo, jnp.concatenate([span, span], axis=0), preferred_element_type=F32)
     for t in range(4):
+        high = lists[4 * s + t : 4 * s + t + 1, :] >> 7
         g = jnp.zeros((8, 128), F32)
         for row in range(16):
-            g = jnp.where(high[t] == row, y[8 * row : 8 * row + 8, 128 * t : 128 * t + 128], g)
+            g = jnp.where(high == row, y[8 * row : 8 * row + 8, 128 * t : 128 * t + 128], g)
         out[8 * t : 8 * t + 8, :] = g
 
 
@@ -321,6 +324,7 @@
     for s in range(4):
         for t in range(4):
             lists[4 * s + t : 4 * s + t + 1, :] = vm[pl.ds(4 * t + towards(s, up[s]), 1), :]
+    mark(lists, onehot)
     for copy in copies[1:]:
         copy.wait()
     for c in range(3):
@@ -486,7 +490,7 @@
 
     def scratch(tiles):
         n = 128 * tiles
-        return [pltpu.VMEM((16, n), F32), pltpu.VMEM((256, n), BF16), pltpu.VMEM((384, n), BF16)]
+        return [pltpu.VMEM((16, n), F32), pltpu.VMEM((128, n), BF16), pltpu.VMEM((384, n), BF16)]
 
     outs = call(
         send_kernel,

time: 22.8 us -> 22.7 us (level)
  Pallas kernels: 6.1 us -> 5.82 us
  transfers between devices with their start and end apart: 8 -> 8, of which waited for: 1 -> 1; matrix products, arithmetic and copies ran while one was open for 0% -> 0% of each run, Pallas kernels for 12% -> 11%
where the time goes in v4:
time: 22.7 us; the launch traced here: 22.3 us
  starting transfers between devices  14 us (62%)
  Pallas kernels  5.82 us (26%)
  waiting for transfers between devices  1.79 us (8%)
  between operations  0.71 us (3%)
    ppermute x8, starting transfers between devices, exchange(): received.append(lax.ppermute(message, ('drift', 'cross'), pairs))  14 us
    ppermute x8, waiting for transfers between devices, exchange(): received.append(lax.ppermute(message, ('drift', 'cross'), pairs))  1.79 us
    pallas_call x1, Pallas kernels, per_device(): call(send_kernel, [shape(48)] * 4 + [shape(a.shape[0], a.dtype, a.shape[1...  1.47 us
    pallas_call x1, Pallas kernels, per_device(): call(own_kernel, [shape(96), shape(48), shape(96), shape(192, BF16, 256)]...  1.47 us
    pallas_call x1, Pallas kernels, per_device(): call(far_kernel, [shape(96)] * 2 + [shape(32)] * 4, scratch(8))  0.93 us
    pallas_call x1, Pallas kernels, per_device(): call(last_kernel, [shape(96), shape(48)])  0.93 us
    pallas_call x1, Pallas kernels, per_device(): call(near_kernel, [shape(96)] + [back] * 2, scratch(8), cost=1 << 30)  0.86 us
  transfers between devices with their start and end apart: 8, of which 1 were waited for; matrix products, arithmetic and copies ran while one was open for 0% of the time, Pallas kernels for 11%

profile of v4, /device:TPU:1, one launch (start us, length us, event | category | flops | bytes accessed | tf_op | source)
XLA Modules:
  0.0 22.3 jit_solution(14739332821852238007)
XLA Ops:
  0.6 1.5 %shard_map.95 = (f32[48,128]{1,0:T(8,128)S(1)}, f32[48,128]{1,0:T(8,128)S(1)}, f32[48,128]{1,0:T(8,128)S(1)}, f32[48,128]{1,0:T(8,128)S(1)}, f32[96,128]{1,0:T(8...) custom-call(f32[96,128]{1,0:T(8,128)} %bitcast.20, ...), custom_call_target="tpu_custom_call" | custom-call | tf_op jit(solution)/shard_map/pallas_call | solution.py:495
  2.1 7.1 %collective-permute-start = (f32[48,128]{1,0:T(8,128)S(1)}, f32[48,128]{1,0:T(8,128)S(1)}, u32[]{:S(2)}, u32[]{:S(2)}) collective-permute-start(f32[48,128]{1,0:T(8,128)S(1)} %get-tuple-element.30), channel_id=1, source_target_pairs={{0,120},{1,121},{2,122},{3,123},{4,124},{5,125},{6,126},{7,127},{8... | collective-permute-start | bytes 73736 | tf_op jit(solution)/shard_map/ppermute | solution.py:474
  9.2 0.0 collective-permute-start.1
  9.2 2.1 %collective-permute-start.2 = (f32[48,128]{1,0:T(8,128)S(1)}, f32[48,128]{1,0:T(8,128)S(1)}, u32[]{:S(2)}, u32[]{:S(2)}) collective-permute-start(f32[48,128]{1,0:T(8,128)S(1)} %get-tuple-element.32), channel_id=1, source_target_pairs={{0,7},{1,2},{2,1},{3,4},{4,3},{5,6},{6,5},{7,0},{8,15},{9,10},{10,... | collective-permute-start | bytes 73736 | tf_op jit(solution)/shard_map/ppermute | solution.py:474
  11.3 0.8 %collective-permute-start.3 = (f32[48,128]{1,0:T(8,128)S(1)}, f32[48,128]{1,0:T(8,128)S(1)}, u32[]{:S(2)}, u32[]{:S(2)}) collective-permute-start(f32[48,128]{1,0:T(8,128)S(1)} %get-tuple-element.33), channel_id=1, source_target_pairs={{0,1},{1,0},{2,3},{3,2},{4,5},{5,4},{6,7},{7,6},{8,9},{9,8},{10,11... | collective-permute-start | bytes 73736 | tf_op jit(solution)/shard_map/ppermute | solution.py:474
  12.1 1.5 %shard_map.96 = (f32[96,128]{1,0:T(8,128)S(1)}, f32[48,128]{1,0:T(8,128)S(1)}, f32[96,128]{1,0:T(8,128)S(1)}, bf16[192,256]{1,0:T(8,128)(2,1)S(1)}) custom-call(f32[96,128]{1,0:T(8,128)S(1)} %get-tuple-element.34.fl, f32[48,128]{1,0:T(8,128)S(1)} %get-tuple-element.35.co, f32[48,128]{1,0:T(8,128)S(1)} %get-tuple-element.36.ve, ...), custom_call_target="tpu_custom_call" | custom-call | flops 2147483648 | tf_op jit(solution)/shard_map/pallas_call | solution.py:510
  13.6 0.0 collective-permute-done.1.r1
  13.6 0.0 collective-permute-done.3.r3
  13.6 0.9 %shard_map.97 = (f32[96,128]{1,0:T(8,128)S(1)}, f32[16,128]{1,0:T(8,128)S(1)}, f32[16,128]{1,0:T(8,128)S(1)}) custom-call(f32[48,128]{1,0:T(8,128)S(1)} %collective-permute-done.1.r1, f32[48,128]{1,0:T(8,128)S(1)} %collective-permute-done.3.r3, bf16[192,256]{1,0:T(8,128)(2,1)S(1)} %get-tuple-element.43.operand, f32[96,128]{1,0:T(8,128)S(1)} %get-tuple-element.44.dep_in), custom_call_target="tpu_custom_call" | custom-call | flops 1073741824 | tf_op jit(solution)/shard_map/pallas_call | solution.py:516
  14.5 0.0 collective-permute-done.r0
  14.5 0.0 collective-permute-done.2.r2
  14.5 0.9 %shard_map.98 = (f32[96,128]{1,0:T(8,128)S(1)}, f32[96,128]{1,0:T(8,128)S(1)}, f32[32,128]{1,0:T(8,128)S(1)}, f32[32,128]{1,0:T(8,128)S(1)}, f32[32,128]{1,0:T(8,128)S(1)}, /*index=5*/f32[32,128]{1,0:T(8,128)S(1)}) custom-call(f32[48,128]{1,0:T(8,128)S(1)} %collective-permute-done.r0, f32[48,128]{1,0:T(8,128)S(1)} %collective-permute-done.1.r1, ...), custom_call_target="tpu_custom_call" | custom-call | tf_op jit(solution)/shard_map/pallas_call | solution.py:517
  15.4 0.8 %collective-permute-start.4 = (f32[32,128]{1,0:T(8,128)S(1)}, f32[32,128]{1,0:T(8,128)S(1)}, u32[]{:S(2)}, u32[]{:S(2)}) collective-permute-start(f32[32,128]{1,0:T(8,128)S(1)} %get-tuple-element.49), channel_id=1, source_target_pairs={{0,120},{1,121},{2,122},{3,123},{4,124},{5,125},{6,126},{7,127},{8... | collective-permute-start | bytes 49160 | tf_op jit(solution)/shard_map/ppermute | solution.py:474
  16.2 0.8 %collective-permute-start.5 = (f32[32,128]{1,0:T(8,128)S(1)}, f32[32,128]{1,0:T(8,128)S(1)}, u32[]{:S(2)}, u32[]{:S(2)}) collective-permute-start(f32[32,128]{1,0:T(8,128)S(1)} %get-tuple-element.50), channel_id=1, source_target_pairs={{0,8},{1,9},{2,10},{3,11},{4,12},{5,13},{6,14},{7,15},{8,0},{9,1},... | collective-permute-start | bytes 49160 | tf_op jit(solution)/shard_map/ppermute | solution.py:474
  17.0 2.4 %collective-permute-start.6 = (f32[32,128]{1,0:T(8,128)S(1)}, f32[32,128]{1,0:T(8,128)S(1)}, u32[]{:S(2)}, u32[]{:S(2)}) collective-permute-start(f32[32,128]{1,0:T(8,128)S(1)} %get-tuple-element.51), channel_id=1, source_target_pairs={{0,7},{1,2},{2,1},{3,4},{4,3},{5,6},{6,5},{7,0},{8,15},{9,10},{10,... | collective-permute-start | bytes 49160 | tf_op jit(solution)/shard_map/ppermute | solution.py:474
  19.4 0.0 collective-permute-start.7
  19.4 0.2 shard_map.99.base
  19.6 1.8 %collective-permute-done.4.r0 = f32[32,128]{1,0:T(8,128)S(1)} collective-permute-done((f32[32,128]{1,0:T(8,128)S(1)}, f32[32,128]{1,0:T(8,128)S(1)}, u32[]{:S(2)}, u32[]{:S(2)}) %collective-permute-start.4) | collective-permute-done | bytes 16416 | tf_op jit(solution)/shard_map/ppermute | solution.py:474
  21.4 0.0 collective-permute-done.5.r1
  21.4 0.0 collective-permute-done.6.r2
  21.4 0.0 collective-permute-done.7.r3
  21.4 0.9 %shard_map.100 = (f32[96,128]{1,0:T(8,128)}, f32[48,128]{1,0:T(8,128)}) custom-call(f32[32,128]{1,0:T(8,128)S(1)} %collective-permute-done.4.r0, f32[32,128]{1,0:T(8,128)S(1)} %collective-permute-done.5.r1, f32[32,128]{1,0:T(8,128)S(1)} %collective-permute-done.6.r2, f32[32,128]{1,0:T(8,128)S(1)} %collective-permute-done.7.r3, ...), custom_call_target="tpu_custom_call" | custom-call | tf_op jit(solution)/shard_map/pallas_call | solution.py:522
Async XLA Ops:
  2.1 12.4 %collective-permute-start = (f32[48,128]{1,0:T(8,128)S(1)}, f32[48,128]{1,0:T(8,128)S(1)}, u32[]{:S(2)}, u32[]{:S(2)}) collective-permute-start(f32[48,128]{1,0:T(8,128)S(1)} %get-tuple-element.30), channel_id=1, source_target_pairs={{0,120},{1,121},{2,122},{3,123},{4,124},{5,125},{6,126},{7,127},{8... | collective-permute-start | bytes 73736 | tf_op jit(solution)/shard_map/ppermute | solution.py:474
  9.2 4.4 %collective-permute-start.1 = (f32[48,128]{1,0:T(8,128)S(1)}, f32[48,128]{1,0:T(8,128)S(1)}, u32[]{:S(2)}, u32[]{:S(2)}) collective-permute-start(f32[48,128]{1,0:T(8,128)S(1)} %get-tuple-element.31), channel_id=1, source_target_pairs={{0,8},{1,9},{2,10},{3,11},{4,12},{5,13},{6,14},{7,15},{8,0},{9,1},... | collective-permute-start | bytes 73736 | tf_op jit(solution)/shard_map/ppermute | solution.py:474
  9.2 5.2 %collective-permute-start.2 = (f32[48,128]{1,0:T(8,128)S(1)}, f32[48,128]{1,0:T(8,128)S(1)}, u32[]{:S(2)}, u32[]{:S(2)}) collective-permute-start(f32[48,128]{1,0:T(8,128)S(1)} %get-tuple-element.32), channel_id=1, source_target_pairs={{0,7},{1,2},{2,1},{3,4},{4,3},{5,6},{6,5},{7,0},{8,15},{9,10},{10,... | collective-permute-start | bytes 73736 | tf_op jit(solution)/shard_map/ppermute | solution.py:474
  11.3 2.3 %collective-permute-start.3 = (f32[48,128]{1,0:T(8,128)S(1)}, f32[48,128]{1,0:T(8,128)S(1)}, u32[]{:S(2)}, u32[]{:S(2)}) collective-permute-start(f32[48,128]{1,0:T(8,128)S(1)} %get-tuple-element.33), channel_id=1, source_target_pairs={{0,1},{1,0},{2,3},{3,2},{4,5},{5,4},{6,7},{7,6},{8,9},{9,8},{10,11... | collective-permute-start | bytes 73736 | tf_op jit(solution)/shard_map/ppermute | solution.py:474
  15.4 6.0 %collective-permute-start.4 = (f32[32,128]{1,0:T(8,128)S(1)}, f32[32,128]{1,0:T(8,128)S(1)}, u32[]{:S(2)}, u32[]{:S(2)}) collective-permute-start(f32[32,128]{1,0:T(8,128)S(1)} %get-tuple-element.49), channel_id=1, source_target_pairs={{0,120},{1,121},{2,122},{3,123},{4,124},{5,125},{6,126},{7,127},{8... | collective-permute-start | bytes 49160 | tf_op jit(solution)/shard_map/ppermute | solution.py:474
  16.2 5.2 %collective-permute-start.5 = (f32[32,128]{1,0:T(8,128)S(1)}, f32[32,128]{1,0:T(8,128)S(1)}, u32[]{:S(2)}, u32[]{:S(2)}) collective-permute-start(f32[32,128]{1,0:T(8,128)S(1)} %get-tuple-element.50), channel_id=1, source_target_pairs={{0,8},{1,9},{2,10},{3,11},{4,12},{5,13},{6,14},{7,15},{8,0},{9,1},... | collective-permute-start | bytes 49160 | tf_op jit(solution)/shard_map/ppermute | solution.py:474
  17.0 4.4 %collective-permute-start.6 = (f32[32,128]{1,0:T(8,128)S(1)}, f32[32,128]{1,0:T(8,128)S(1)}, u32[]{:S(2)}, u32[]{:S(2)}) collective-permute-start(f32[32,128]{1,0:T(8,128)S(1)} %get-tuple-element.51), channel_id=1, source_target_pairs={{0,7},{1,2},{2,1},{3,4},{4,3},{5,6},{6,5},{7,0},{8,15},{9,10},{10,... | collective-permute-start | bytes 49160 | tf_op jit(solution)/shard_map/ppermute | solution.py:474
  19.4 2.0 %collective-permute-start.7 = (f32[32,128]{1,0:T(8,128)S(1)}, f32[32,128]{1,0:T(8,128)S(1)}, u32[]{:S(2)}, u32[]{:S(2)}) collective-permute-start(f32[32,128]{1,0:T(8,128)S(1)} %get-tuple-element.52), channel_id=1, source_target_pairs={{0,1},{1,0},{2,3},{3,2},{4,5},{5,4},{6,7},{7,6},{8,9},{9,8},{10,11... | collective-permute-start | bytes 49160 | tf_op jit(solution)/shard_map/ppermute | solution.py:474

commit v5 on v4

--- a/solution.py
+++ b/solution.py
@@ -325,7 +325,7 @@
         for t in range(4):
             lists[4 * s + t : 4 * s + t + 1, :] = vm[pl.ds(4 * t + towards(s, up[s]), 1), :]
     mark(lists, onehot)
-    for copy in copies[1:]:
+    for copy in copies[1:6]:
         copy.wait()
     for c in range(3):
         table[pl.ds(c, 16, stride=8), :] = vc[16 * c : 16 * c + 16, :]
@@ -337,6 +337,8 @@
     for s, out in enumerate((o0, o1, o2, o3)):
         out[FACES:, :] = faces_to(s, up[s], packed)
         gather(s, parts, lists, onehot, out)
+    for copy in copies[6:]:
+        copy.wait()
 
 
 def own_kernel(

time: 22.7 us -> 22.6 us (level)
  no operation moved by 1% of the time
where the time goes in v5:
time: 22.6 us; the launch traced here: 22.2 us
  starting transfers between devices  14 us (62%)
  Pallas kernels  5.68 us (25%)
  waiting for transfers between devices  1.79 us (8%)
  between operations  0.71 us (3%)
    ppermute x8, starting transfers between devices, exchange(): received.append(lax.ppermute(message, ('drift', 'cross'), pairs))  14 us
    ppermute x8, waiting for transfers between devices, exchange(): received.append(lax.ppermute(message, ('drift', 'cross'), pairs))  1.79 us
    pallas_call x1, Pallas kernels, per_device(): call(own_kernel, [shape(96), shape(48), shape(96), shape(192, BF16, 256)]...  1.47 us
    pallas_call x1, Pallas kernels, per_device(): call(send_kernel, [shape(48)] * 4 + [shape(a.shape[0], a.dtype, a.shape[1...  1.33 us
    pallas_call x1, Pallas kernels, per_device(): call(far_kernel, [shape(96)] * 2 + [shape(32)] * 4, scratch(8))  0.93 us
    pallas_call x1, Pallas kernels, per_device(): call(last_kernel, [shape(96), shape(48)])  0.93 us
    pallas_call x1, Pallas kernels, per_device(): call(near_kernel, [shape(96)] + [back] * 2, scratch(8), cost=1 << 30)  0.86 us
  transfers between devices with their start and end apart: 8, of which 1 were waited for; matrix products, arithmetic and copies ran while one was open for 0% of the time, Pallas kernels for 11%

profile of v5, /device:TPU:1, one launch (start us, length us, event | category | flops | bytes accessed | tf_op | source)
XLA Modules:
  0.0 22.2 jit_solution(3034486223465759956)
XLA Ops:
  0.6 1.3 %shard_map.95 = (f32[48,128]{1,0:T(8,128)S(1)}, f32[48,128]{1,0:T(8,128)S(1)}, f32[48,128]{1,0:T(8,128)S(1)}, f32[48,128]{1,0:T(8,128)S(1)}, f32[96,128]{1,0:T(8...) custom-call(f32[96,128]{1,0:T(8,128)} %bitcast.20, ...), custom_call_target="tpu_custom_call" | custom-call | tf_op jit(solution)/shard_map/pallas_call | solution.py:497
  2.0 7.1 %collective-permute-start = (f32[48,128]{1,0:T(8,128)S(1)}, f32[48,128]{1,0:T(8,128)S(1)}, u32[]{:S(2)}, u32[]{:S(2)}) collective-permute-start(f32[48,128]{1,0:T(8,128)S(1)} %get-tuple-element.30), channel_id=1, source_target_pairs={{0,120},{1,121},{2,122},{3,123},{4,124},{5,125},{6,126},{7,127},{8... | collective-permute-start | bytes 73736 | tf_op jit(solution)/shard_map/ppermute | solution.py:476
  9.1 0.0 collective-permute-start.1
  9.1 2.1 %collective-permute-start.2 = (f32[48,128]{1,0:T(8,128)S(1)}, f32[48,128]{1,0:T(8,128)S(1)}, u32[]{:S(2)}, u32[]{:S(2)}) collective-permute-start(f32[48,128]{1,0:T(8,128)S(1)} %get-tuple-element.32), channel_id=1, source_target_pairs={{0,7},{1,2},{2,1},{3,4},{4,3},{5,6},{6,5},{7,0},{8,15},{9,10},{10,... | collective-permute-start | bytes 73736 | tf_op jit(solution)/shard_map/ppermute | solution.py:476
  11.1 0.8 %collective-permute-start.3 = (f32[48,128]{1,0:T(8,128)S(1)}, f32[48,128]{1,0:T(8,128)S(1)}, u32[]{:S(2)}, u32[]{:S(2)}) collective-permute-start(f32[48,128]{1,0:T(8,128)S(1)} %get-tuple-element.33), channel_id=1, source_target_pairs={{0,1},{1,0},{2,3},{3,2},{4,5},{5,4},{6,7},{7,6},{8,9},{9,8},{10,11... | collective-permute-start | bytes 73736 | tf_op jit(solution)/shard_map/ppermute | solution.py:476
  12.0 1.5 %shard_map.96 = (f32[96,128]{1,0:T(8,128)S(1)}, f32[48,128]{1,0:T(8,128)S(1)}, f32[96,128]{1,0:T(8,128)S(1)}, bf16[192,256]{1,0:T(8,128)(2,1)S(1)}) custom-call(f32[96,128]{1,0:T(8,128)S(1)} %get-tuple-element.34.fl, f32[48,128]{1,0:T(8,128)S(1)} %get-tuple-element.35.co, f32[48,128]{1,0:T(8,128)S(1)} %get-tuple-element.36.ve, ...), custom_call_target="tpu_custom_call" | custom-call | flops 2147483648 | tf_op jit(solution)/shard_map/pallas_call | solution.py:512
  13.4 0.0 collective-permute-done.1.r1
  13.4 0.0 collective-permute-done.3.r3
  13.4 0.9 %shard_map.97 = (f32[96,128]{1,0:T(8,128)S(1)}, f32[16,128]{1,0:T(8,128)S(1)}, f32[16,128]{1,0:T(8,128)S(1)}) custom-call(f32[48,128]{1,0:T(8,128)S(1)} %collective-permute-done.1.r1, f32[48,128]{1,0:T(8,128)S(1)} %collective-permute-done.3.r3, bf16[192,256]{1,0:T(8,128)(2,1)S(1)} %get-tuple-element.43.operand, f32[96,128]{1,0:T(8,128)S(1)} %get-tuple-element.44.dep_in), custom_call_target="tpu_custom_call" | custom-call | flops 1073741824 | tf_op jit(solution)/shard_map/pallas_call | solution.py:518
  14.3 0.0 collective-permute-done.r0
  14.3 0.0 collective-permute-done.2.r2
  14.3 0.9 %shard_map.98 = (f32[96,128]{1,0:T(8,128)S(1)}, f32[96,128]{1,0:T(8,128)S(1)}, f32[32,128]{1,0:T(8,128)S(1)}, f32[32,128]{1,0:T(8,128)S(1)}, f32[32,128]{1,0:T(8,128)S(1)}, /*index=5*/f32[32,128]{1,0:T(8,128)S(1)}) custom-call(f32[48,128]{1,0:T(8,128)S(1)} %collective-permute-done.r0, f32[48,128]{1,0:T(8,128)S(1)} %collective-permute-done.1.r1, ...), custom_call_target="tpu_custom_call" | custom-call | tf_op jit(solution)/shard_map/pallas_call | solution.py:519
  15.3 0.8 %collective-permute-start.4 = (f32[32,128]{1,0:T(8,128)S(1)}, f32[32,128]{1,0:T(8,128)S(1)}, u32[]{:S(2)}, u32[]{:S(2)}) collective-permute-start(f32[32,128]{1,0:T(8,128)S(1)} %get-tuple-element.49), channel_id=1, source_target_pairs={{0,120},{1,121},{2,122},{3,123},{4,124},{5,125},{6,126},{7,127},{8... | collective-permute-start | bytes 49160 | tf_op jit(solution)/shard_map/ppermute | solution.py:476
  16.1 0.8 %collective-permute-start.5 = (f32[32,128]{1,0:T(8,128)S(1)}, f32[32,128]{1,0:T(8,128)S(1)}, u32[]{:S(2)}, u32[]{:S(2)}) collective-permute-start(f32[32,128]{1,0:T(8,128)S(1)} %get-tuple-element.50), channel_id=1, source_target_pairs={{0,8},{1,9},{2,10},{3,11},{4,12},{5,13},{6,14},{7,15},{8,0},{9,1},... | collective-permute-start | bytes 49160 | tf_op jit(solution)/shard_map/ppermute | solution.py:476
  16.9 2.4 %collective-permute-start.6 = (f32[32,128]{1,0:T(8,128)S(1)}, f32[32,128]{1,0:T(8,128)S(1)}, u32[]{:S(2)}, u32[]{:S(2)}) collective-permute-start(f32[32,128]{1,0:T(8,128)S(1)} %get-tuple-element.51), channel_id=1, source_target_pairs={{0,7},{1,2},{2,1},{3,4},{4,3},{5,6},{6,5},{7,0},{8,15},{9,10},{10,... | collective-permute-start | bytes 49160 | tf_op jit(solution)/shard_map/ppermute | solution.py:476
  19.3 0.0 collective-permute-start.7
  19.3 0.2 shard_map.99.base
  19.5 1.8 %collective-permute-done.4.r0 = f32[32,128]{1,0:T(8,128)S(1)} collective-permute-done((f32[32,128]{1,0:T(8,128)S(1)}, f32[32,128]{1,0:T(8,128)S(1)}, u32[]{:S(2)}, u32[]{:S(2)}) %collective-permute-start.4) | collective-permute-done | bytes 16416 | tf_op jit(solution)/shard_map/ppermute | solution.py:476
  21.3 0.0 collective-permute-done.5.r1
  21.3 0.0 collective-permute-done.6.r2
  21.3 0.0 collective-permute-done.7.r3
  21.3 0.9 %shard_map.100 = (f32[96,128]{1,0:T(8,128)}, f32[48,128]{1,0:T(8,128)}) custom-call(f32[32,128]{1,0:T(8,128)S(1)} %collective-permute-done.4.r0, f32[32,128]{1,0:T(8,128)S(1)} %collective-permute-done.5.r1, f32[32,128]{1,0:T(8,128)S(1)} %collective-permute-done.6.r2, f32[32,128]{1,0:T(8,128)S(1)} %collective-permute-done.7.r3, ...), custom_call_target="tpu_custom_call" | custom-call | tf_op jit(solution)/shard_map/pallas_call | solution.py:524
Async XLA Ops:
  2.0 12.4 %collective-permute-start = (f32[48,128]{1,0:T(8,128)S(1)}, f32[48,128]{1,0:T(8,128)S(1)}, u32[]{:S(2)}, u32[]{:S(2)}) collective-permute-start(f32[48,128]{1,0:T(8,128)S(1)} %get-tuple-element.30), channel_id=1, source_target_pairs={{0,120},{1,121},{2,122},{3,123},{4,124},{5,125},{6,126},{7,127},{8... | collective-permute-start | bytes 73736 | tf_op jit(solution)/shard_map/ppermute | solution.py:476
  9.1 4.4 %collective-permute-start.1 = (f32[48,128]{1,0:T(8,128)S(1)}, f32[48,128]{1,0:T(8,128)S(1)}, u32[]{:S(2)}, u32[]{:S(2)}) collective-permute-start(f32[48,128]{1,0:T(8,128)S(1)} %get-tuple-element.31), channel_id=1, source_target_pairs={{0,8},{1,9},{2,10},{3,11},{4,12},{5,13},{6,14},{7,15},{8,0},{9,1},... | collective-permute-start | bytes 73736 | tf_op jit(solution)/shard_map/ppermute | solution.py:476
  9.1 5.2 %collective-permute-start.2 = (f32[48,128]{1,0:T(8,128)S(1)}, f32[48,128]{1,0:T(8,128)S(1)}, u32[]{:S(2)}, u32[]{:S(2)}) collective-permute-start(f32[48,128]{1,0:T(8,128)S(1)} %get-tuple-element.32), channel_id=1, source_target_pairs={{0,7},{1,2},{2,1},{3,4},{4,3},{5,6},{6,5},{7,0},{8,15},{9,10},{10,... | collective-permute-start | bytes 73736 | tf_op jit(solution)/shard_map/ppermute | solution.py:476
  11.1 2.3 %collective-permute-start.3 = (f32[48,128]{1,0:T(8,128)S(1)}, f32[48,128]{1,0:T(8,128)S(1)}, u32[]{:S(2)}, u32[]{:S(2)}) collective-permute-start(f32[48,128]{1,0:T(8,128)S(1)} %get-tuple-element.33), channel_id=1, source_target_pairs={{0,1},{1,0},{2,3},{3,2},{4,5},{5,4},{6,7},{7,6},{8,9},{9,8},{10,11... | collective-permute-start | bytes 73736 | tf_op jit(solution)/shard_map/ppermute | solution.py:476
  15.3 6.0 %collective-permute-start.4 = (f32[32,128]{1,0:T(8,128)S(1)}, f32[32,128]{1,0:T(8,128)S(1)}, u32[]{:S(2)}, u32[]{:S(2)}) collective-permute-start(f32[32,128]{1,0:T(8,128)S(1)} %get-tuple-element.49), channel_id=1, source_target_pairs={{0,120},{1,121},{2,122},{3,123},{4,124},{5,125},{6,126},{7,127},{8... | collective-permute-start | bytes 49160 | tf_op jit(solution)/shard_map/ppermute | solution.py:476
  16.1 5.2 %collective-permute-start.5 = (f32[32,128]{1,0:T(8,128)S(1)}, f32[32,128]{1,0:T(8,128)S(1)}, u32[]{:S(2)}, u32[]{:S(2)}) collective-permute-start(f32[32,128]{1,0:T(8,128)S(1)} %get-tuple-element.50), channel_id=1, source_target_pairs={{0,8},{1,9},{2,10},{3,11},{4,12},{5,13},{6,14},{7,15},{8,0},{9,1},... | collective-permute-start | bytes 49160 | tf_op jit(solution)/shard_map/ppermute | solution.py:476
  16.9 4.4 %collective-permute-start.6 = (f32[32,128]{1,0:T(8,128)S(1)}, f32[32,128]{1,0:T(8,128)S(1)}, u32[]{:S(2)}, u32[]{:S(2)}) collective-permute-start(f32[32,128]{1,0:T(8,128)S(1)} %get-tuple-element.51), channel_id=1, source_target_pairs={{0,7},{1,2},{2,1},{3,4},{4,3},{5,6},{6,5},{7,0},{8,15},{9,10},{10,... | collective-permute-start | bytes 49160 | tf_op jit(solution)/shard_map/ppermute | solution.py:476
  19.3 2.0 %collective-permute-start.7 = (f32[32,128]{1,0:T(8,128)S(1)}, f32[32,128]{1,0:T(8,128)S(1)}, u32[]{:S(2)}, u32[]{:S(2)}) collective-permute-start(f32[32,128]{1,0:T(8,128)S(1)} %get-tuple-element.52), channel_id=1, source_target_pairs={{0,1},{1,0},{2,3},{3,2},{4,5},{5,4},{6,7},{7,6},{8,9},{9,8},{10,11... | collective-permute-start | bytes 49160 | tf_op jit(solution)/shard_map/ppermute | solution.py:476
